TPU v7x, 32 devices: a whole 2x2x4 slice. The times are simulated.
32 devices in a mesh: ctx: 16 (over z, y, core), head: 2 (over x).
Axes of the slice: x: 2, y: 2, z: 4, core: 2. Of those that a mesh axis runs over, the one named last changes fastest.
Arguments:
- queries: bfloat16 [12288, 2048], P('ctx', 'head')
- keys: bfloat16 [12288, 2048], P('ctx', 'head')
- values: bfloat16 [12288, 2048], P('ctx', 'head'), may hold values from -6 to 6
- w_out: bfloat16 [2048, 2048], P('head'), may hold values from -2.5 to 2.5
Outputs:
- layer_out: bfloat16 [12288, 2048], P('ctx', 'head')
All inputs are finite; a program needn't handle non-finite values.
Results may differ from a plain program's by a relative error of at most 0.0067.
Values may be sent and summed in bfloat16 or wider, within the bound.
No kernel may reach another device: no remote copies, remote signals or barrier semaphores. Data moves between devices by JAX's collectives and lax.ppermute only.
A program may use at most 64 MiB of HBM per device.

v0:
```python
import math

import jax
import jax.numpy as jnp
from jax import lax
from jax.sharding import PartitionSpec as P

HD = 128
BLOCK = 256
SUMS = 16


NEG_FILL = -1e30


def shifted(value, axis, steps):
    count = lax.axis_size(axis)
    first, last = (max(0, -steps), min(count, count - steps))
    return lax.ppermute(value, axis, [(source, source + steps) for source in range(first, last)])


def per_device(queries, keys, values, w_out):
    tok_rows, feat_width = queries.shape
    head_count = feat_width // HD
    score_scale = 1.0 / math.sqrt(HD)
    blocks = tok_rows // BLOCK
    per_shard = blocks * SUMS
    tail_rows = jnp.stack([keys[tok_rows - BLOCK :], values[tok_rows - BLOCK :]])
    band_rim = shifted(tail_rows, "ctx", 1)
    own_sums = jnp.stack(
        [
            keys.reshape(blocks, BLOCK, feat_width)[:, BLOCK - SUMS :, :].reshape(
                per_shard, feat_width
            ),
            values.reshape(blocks, BLOCK, feat_width)[:, BLOCK - SUMS :, :].reshape(
                per_shard, feat_width
            ),
        ]
    )
    all_sums = lax.all_gather(own_sums, "ctx", axis=1, tiled=True)
    first_row = lax.axis_index("ctx") * tok_rows
    band_keys = jnp.concatenate([band_rim[0], keys], axis=0)
    band_values = jnp.concatenate([band_rim[1], values], axis=0)
    query_pos = first_row + jnp.arange(tok_rows, dtype=jnp.int32)
    key_pos = first_row - BLOCK + jnp.arange(tok_rows + BLOCK, dtype=jnp.int32)
    band_ok = (key_pos[None, :] <= query_pos[:, None]) & (
        key_pos[None, :] > query_pos[:, None] - BLOCK
    )
    sum_index = jnp.arange(all_sums.shape[1], dtype=jnp.int32)
    sum_pos = sum_index // SUMS * BLOCK + BLOCK - SUMS + sum_index % SUMS
    sum_ok = sum_pos[None, :] <= query_pos[:, None] - BLOCK
    contract = (((1,), (1,)), ((), ()))

    def one_head(head_id):
        head_start = head_id * HD
        query_head = lax.dynamic_slice_in_dim(queries, head_start, HD, 1)
        band_key = lax.dynamic_slice_in_dim(band_keys, head_start, HD, 1)
        band_value = lax.dynamic_slice_in_dim(band_values, head_start, HD, 1)
        sum_key = lax.dynamic_slice_in_dim(all_sums[0], head_start, HD, 1)
        sum_value = lax.dynamic_slice_in_dim(all_sums[1], head_start, HD, 1)
        band_score = (
            lax.dot_general(query_head, band_key, contract, preferred_element_type=jnp.float32)
            * score_scale
        )
        sum_score = (
            lax.dot_general(query_head, sum_key, contract, preferred_element_type=jnp.float32)
            * score_scale
        )
        band_score = jnp.where(band_ok, band_score, NEG_FILL)
        sum_score = jnp.where(sum_ok, sum_score, NEG_FILL)
        row_max = jnp.maximum(
            jnp.max(band_score, axis=1, keepdims=True), jnp.max(sum_score, axis=1, keepdims=True)
        )
        band_exp = jnp.where(band_ok, jnp.exp(band_score - row_max), 0.0)
        sum_exp = jnp.where(sum_ok, jnp.exp(sum_score - row_max), 0.0)
        total = jnp.sum(band_exp, axis=1, keepdims=True) + jnp.sum(sum_exp, axis=1, keepdims=True)
        band_weight = (band_exp / total).astype(jnp.bfloat16)
        sum_weight = (sum_exp / total).astype(jnp.bfloat16)
        mixed = jnp.dot(band_weight, band_value, preferred_element_type=jnp.float32)
        mixed = mixed + jnp.dot(sum_weight, sum_value, preferred_element_type=jnp.float32)
        return mixed.astype(jnp.bfloat16)

    head_outs = lax.map(one_head, jnp.arange(head_count, dtype=jnp.int32))
    attended = head_outs.transpose(1, 0, 2).reshape(tok_rows, feat_width)
    summed = lax.psum_scatter(
        lax.dot_general(
            w_out, attended, (((0,), (1,)), ((), ())), preferred_element_type=jnp.float32
        ).astype(jnp.bfloat16),
        "head",
        scatter_dimension=0,
        tiled=True,
    ).astype(jnp.float32)
    return summed.T.astype(jnp.bfloat16)


def solution(mesh):
    in_specs = (P("ctx", "head"), P("ctx", "head"), P("ctx", "head"), P("head", None))
    out_specs = P("ctx", "head")
    return jax.shard_map(
        per_device, mesh=mesh, in_specs=in_specs, out_specs=out_specs, check_vma=False
    )
```

profile of v0, /device:TPU:26, one launch (start us, length us, event | category | flops | bytes accessed | tf_op | source)
XLA Modules:
  0.0 221.0 jit_solution(8086894138173776464)
XLA Ops:
  6.5 0.9 slice.36
  7.4 0.9 slice.35
  9.1 1.3 slice_bitcast_fusion.2
  10.4 1.1 pad_maximum_fusion.2
  11.5 1.9 collective-permute-start
  13.4 21.6 %collective-permute-done = bf16[2,256,1024]{2,1,0:T(8,128)(2,1)S(1)} collective-permute-done((bf16[2,256,1024]{2,1,0:T(8,128)(2,1)}, bf16[2,256,1024]{2,1,0:T(8,128)(2,1)S(1)}, u32[]{:S(2)}, u32[]{:S(2)}) %collective-permute-start) | collective-permute-done | bytes 1048608 | tf_op jit(solution)/shard_map/ppermute | solution.py:19
  35.1 1.5 pad_maximum_fusion.1
  37.3 18.3 %all-gather.2.cloned.1.call-done = bf16[2,768,1024]{2,1,0:T(8,128)(2,1)} async-done(((bf16[2,48,1024]{2,1,0:T(8,128)(2,1)}), bf16[2,768,1024]{2,1,0:T(8,128)(2,1)}) %all-gather.2.cloned.1.call-update) | async-done | bytes 3145744 | tf_op jit(solution)/shard_map/all_gather | solution.py:40
  55.6 108.1 %while.12 = (s32[]{:T(128)}, bf16[8,768,128]{1,2,0:T(8,128)(2,1)}, s32[8]{0:T(128)S(1)}, bf16[768,1024]{1,0:T(8,128)(2,1)}, bf16[1024,1024]{1,0:T(8,128)(2,1)S(1...) while((s32[]{:T(128)}, bf16[8,768,128]{1,2,0:T(8,128)(2,1)}, ...), condition=%wide.region_5.6_spmd.clone.clone, body=%wide.region_0.5_spmd.clone.clone.sunk | while | flops 732953088 | bytes 25995484 | solution.py:83
  57.0 2.2 fusion.57
  59.2 1.4 fusion.58
  60.6 2.3 %fusion.56 = (f32[768]{0:T(1024)S(1)}, f32[768,1024]{1,0:T(8,128)S(1)}) fusion(s32[1024]{0:T(1024)S(1)} %get-tuple-element.264, s32[768]{0:T(1024)S(1)} %get-tuple-element.263, s32[768]{0:T(1024)S(1)} %get-tuple-element.262, bf16[1024,1024]{1,0:T(8,128)(2,1)S(1)} %get-tuple-element.259, s32[]{:T(128)S(6)} %select_n.124, ...), kind=kOutput, calls=%fused_computation.8.clone.1 | convolution fusion | flops 206044416 | bytes 3620864 | tf_op jit(solution)/shard_map/while/body/eval_jaxpr/dot_general | solution.py:62
  63.6 1.5 fusion.59
  65.1 2.2 fusion.61
  67.3 1.0 fusion.62
  68.5 0.7 constant_dynamic-update-slice_fusion.2
  70.5 2.2 fusion.57
  72.7 1.4 fusion.58
  74.2 2.3 %fusion.56 = (f32[768]{0:T(1024)S(1)}, f32[768,1024]{1,0:T(8,128)S(1)}) fusion(s32[1024]{0:T(1024)S(1)} %get-tuple-element.264, s32[768]{0:T(1024)S(1)} %get-tuple-element.263, s32[768]{0:T(1024)S(1)} %get-tuple-element.262, bf16[1024,1024]{1,0:T(8,128)(2,1)S(1)} %get-tuple-element.259, s32[]{:T(128)S(6)} %select_n.124, ...), kind=kOutput, calls=%fused_computation.8.clone.1 | convolution fusion | flops 206044416 | bytes 3620864 | tf_op jit(solution)/shard_map/while/body/eval_jaxpr/dot_general | solution.py:62
  77.1 1.5 fusion.59
  78.7 2.2 fusion.61
  80.8 1.0 fusion.62
  84.0 2.2 fusion.57
  86.2 1.4 fusion.58
  87.7 2.3 %fusion.56 = (f32[768]{0:T(1024)S(1)}, f32[768,1024]{1,0:T(8,128)S(1)}) fusion(s32[1024]{0:T(1024)S(1)} %get-tuple-element.264, s32[768]{0:T(1024)S(1)} %get-tuple-element.263, s32[768]{0:T(1024)S(1)} %get-tuple-element.262, bf16[1024,1024]{1,0:T(8,128)(2,1)S(1)} %get-tuple-element.259, s32[]{:T(128)S(6)} %select_n.124, ...), kind=kOutput, calls=%fused_computation.8.clone.1 | convolution fusion | flops 206044416 | bytes 3620864 | tf_op jit(solution)/shard_map/while/body/eval_jaxpr/dot_general | solution.py:62
  90.6 1.5 fusion.59
  92.2 2.2 fusion.61
  94.3 1.0 fusion.62
  95.5 0.7 constant_dynamic-update-slice_fusion.2
  97.5 2.2 fusion.57
  99.7 1.4 fusion.58
  101.2 2.3 %fusion.56 = (f32[768]{0:T(1024)S(1)}, f32[768,1024]{1,0:T(8,128)S(1)}) fusion(s32[1024]{0:T(1024)S(1)} %get-tuple-element.264, s32[768]{0:T(1024)S(1)} %get-tuple-element.263, s32[768]{0:T(1024)S(1)} %get-tuple-element.262, bf16[1024,1024]{1,0:T(8,128)(2,1)S(1)} %get-tuple-element.259, s32[]{:T(128)S(6)} %select_n.124, ...), kind=kOutput, calls=%fused_computation.8.clone.1 | convolution fusion | flops 206044416 | bytes 3620864 | tf_op jit(solution)/shard_map/while/body/eval_jaxpr/dot_general | solution.py:62
  104.2 1.5 fusion.59
  105.7 2.2 fusion.61
  107.8 1.0 fusion.62
  111.1 2.2 fusion.57
  113.2 1.4 fusion.58
  114.7 2.3 %fusion.56 = (f32[768]{0:T(1024)S(1)}, f32[768,1024]{1,0:T(8,128)S(1)}) fusion(s32[1024]{0:T(1024)S(1)} %get-tuple-element.264, s32[768]{0:T(1024)S(1)} %get-tuple-element.263, s32[768]{0:T(1024)S(1)} %get-tuple-element.262, bf16[1024,1024]{1,0:T(8,128)(2,1)S(1)} %get-tuple-element.259, s32[]{:T(128)S(6)} %select_n.124, ...), kind=kOutput, calls=%fused_computation.8.clone.1 | convolution fusion | flops 206044416 | bytes 3620864 | tf_op jit(solution)/shard_map/while/body/eval_jaxpr/dot_general | solution.py:62
  117.7 1.5 fusion.59
  119.2 2.2 fusion.61
  121.4 1.0 fusion.62
  122.5 0.7 constant_dynamic-update-slice_fusion.2
  124.6 2.2 fusion.57
  126.8 1.4 fusion.58
  128.2 2.3 %fusion.56 = (f32[768]{0:T(1024)S(1)}, f32[768,1024]{1,0:T(8,128)S(1)}) fusion(s32[1024]{0:T(1024)S(1)} %get-tuple-element.264, s32[768]{0:T(1024)S(1)} %get-tuple-element.263, s32[768]{0:T(1024)S(1)} %get-tuple-element.262, bf16[1024,1024]{1,0:T(8,128)(2,1)S(1)} %get-tuple-element.259, s32[]{:T(128)S(6)} %select_n.124, ...), kind=kOutput, calls=%fused_computation.8.clone.1 | convolution fusion | flops 206044416 | bytes 3620864 | tf_op jit(solution)/shard_map/while/body/eval_jaxpr/dot_general | solution.py:62
  131.2 1.5 fusion.59
  132.7 2.2 fusion.61
  134.9 1.0 fusion.62
  136.0 0.7 constant_dynamic-update-slice_fusion.2
  138.1 2.2 fusion.57
  140.3 1.4 fusion.58
  141.7 2.3 %fusion.56 = (f32[768]{0:T(1024)S(1)}, f32[768,1024]{1,0:T(8,128)S(1)}) fusion(s32[1024]{0:T(1024)S(1)} %get-tuple-element.264, s32[768]{0:T(1024)S(1)} %get-tuple-element.263, s32[768]{0:T(1024)S(1)} %get-tuple-element.262, bf16[1024,1024]{1,0:T(8,128)(2,1)S(1)} %get-tuple-element.259, s32[]{:T(128)S(6)} %select_n.124, ...), kind=kOutput, calls=%fused_computation.8.clone.1 | convolution fusion | flops 206044416 | bytes 3620864 | tf_op jit(solution)/shard_map/while/body/eval_jaxpr/dot_general | solution.py:62
  144.7 1.5 fusion.59
  146.2 2.2 fusion.61
  148.4 1.0 fusion.62
  149.5 0.7 constant_dynamic-update-slice_fusion.2
  151.6 2.2 fusion.57
  153.8 1.4 fusion.58
  155.2 2.3 %fusion.56 = (f32[768]{0:T(1024)S(1)}, f32[768,1024]{1,0:T(8,128)S(1)}) fusion(s32[1024]{0:T(1024)S(1)} %get-tuple-element.264, s32[768]{0:T(1024)S(1)} %get-tuple-element.263, s32[768]{0:T(1024)S(1)} %get-tuple-element.262, bf16[1024,1024]{1,0:T(8,128)(2,1)S(1)} %get-tuple-element.259, s32[]{:T(128)S(6)} %select_n.124, ...), kind=kOutput, calls=%fused_computation.8.clone.1 | convolution fusion | flops 206044416 | bytes 3620864 | tf_op jit(solution)/shard_map/while/body/eval_jaxpr/dot_general | solution.py:62
  158.2 1.5 fusion.59
  159.7 2.2 fusion.61
  161.9 1.0 fusion.62
  163.7 7.8 %fusion.31 = bf16[2048,768]{0,1:T(8,128)(2,1)} fusion(bf16[768,1024]{0,1:T(8,128)(2,1)} %bitcast.43, bf16[1024,2048]{1,0:T(8,128)(2,1)} %param.9), kind=kOutput, calls=%fused_computation.39 | convolution fusion | flops 3222798336 | bytes 8912896 | tf_op jit(solution)/shard_map/dot_general | solution.py:86
  171.6 42.6 %reduce-scatter.2.cloned.1.call-done = bf16[1024,768]{0,1:T(8,128)(2,1)} async-done(((bf16[2048,768]{0,1:T(8,128)(2,1)}), bf16[1024,768]{0,1:T(8,128)(2,1)}) %reduce-scatter.2.cloned.1.call-update) | async-done | bytes 1572880 | tf_op jit(solution)/shard_map/reduce_scatter | solution.py:85
  (59 shorter events, 15.7 us)
Async XLA Ops:
  6.5 49.1 %all-gather.2.cloned.1.call-start = ((), (), s32[]{:S(2)}) async-start(), calls=%async_computation.1 | async-start | bytes 3342336 | tf_op jit(solution)/shard_map/all_gather | solution.py:40
  9.1 205.1 %reduce-scatter.2.cloned.1.call-start = ((), (), s32[]{:S(2)}) async-start(), calls=%async_computation.2 | async-start | bytes 4718592 | tf_op jit(solution)/shard_map/reduce_scatter | solution.py:85
  10.4 24.7 %copy-start = (bf16[768,1024]{1,0:T(8,128)(2,1)S(1)}, bf16[768,1024]{1,0:T(8,128)(2,1)}, u32[]{:S(2)}) copy-start(bf16[768,1024]{1,0:T(8,128)(2,1)} %param.8) | copy-start | bytes 4718596
  11.5 23.5 %collective-permute-start = (bf16[2,256,1024]{2,1,0:T(8,128)(2,1)}, bf16[2,256,1024]{2,1,0:T(8,128)(2,1)S(1)}, u32[]{:S(2)}, u32[]{:S(2)}) collective-permute-start(bf16[2,256,1024]{2,1,0:T(8,128)(2,1)} %pad_maximum_fusion.2), channel_id=1, source_target_pairs={{0,2},{2,4},{4,6},{6,8},{8,10},{10,12},{12,14},{14,16},{16,18},{18... | collective-permute-start | bytes 3145736 | tf_op jit(solution)/shard_map/ppermute | solution.py:19
  35.1 2.1 copy-start.1
Sparse Core Ops, SparseCore 0:
  9.6 45.9 all-gather.1
  171.7 42.4 reduce-scatter.1
where the time goes:
time: 225 us; the launch traced here: 221 us
  waiting for transfers between devices  82.5 us (37%)
  matrix products  62.6 us (28%)
  local copies, waits for them, and re-layouts  33.2 us (15%)
  other arithmetic  21.1 us (9%)
  between operations  13.5 us (6%)
  loops' own time  6.16 us (3%)
    reduce_scatter x1, waiting for transfers between devices, per_device(): lax.psum_scatter(lax.dot_general(w_out, attended, (((0,), (1,)), ((), ())...  42.6 us
    ppermute x1, waiting for transfers between devices, shifted(): lax.ppermute(value, axis, [(source, source + steps) for source in range(f...  21.6 us
    all_gather x1, waiting for transfers between devices, per_device(): all_sums = lax.all_gather(own_sums, 'ctx', axis=1, tiled=True)  18.3 us
    dot_general x8, matrix products, one_head(): lax.dot_general(query_head, band_key, contract, preferred_element_type=jn...  18.1 us
    slice x8, local copies, waits for them, and re-layouts, one_head(): sum_value = lax.dynamic_slice_in_dim(all_sums[1], head_start, HD, 1)  17.5 us
    dot_general x8, matrix products, one_head(): mixed = jnp.dot(band_weight, band_value, preferred_element_type=jnp.float32)  17.3 us
    reduce_sum x8, other arithmetic, one_head(): jnp.sum(band_exp, axis=1, keepdims=True)  12 us
    dot_general x8, matrix products, one_head(): lax.dot_general(query_head, sum_key, contract, preferred_element_type=jnp...  11.5 us
  transfers between devices with their start and end apart: 3, of which 3 were waited for; matrix products, arithmetic and copies ran while one was open for 2% of the time, Pallas kernels for 0%

commit v1 on v0

v1 whole, which is shorter than its diff:
```python
import functools
import math

import jax
import jax.numpy as jnp
from jax import lax
from jax.experimental import pallas as pl
from jax.experimental.pallas import tpu as pltpu
from jax.sharding import PartitionSpec as P

HD = 128
BLOCK = 256
SUMS = 16
NEG = -3.3e38
SCALE2 = math.log2(math.e) / math.sqrt(HD)


def attend_kernel(pieces, info_ref, q_ref, kp_ref, vp_ref, k_ref, v_ref, bias_ref, *rest):
    sums, out_ref = rest[:pieces], rest[pieces]
    q = q_ref[...]
    nt = (((1,), (1,)), ((), ()))
    per = sums[0].shape[0] // 2
    k_sum = jnp.concatenate([s[0:per, :] for s in sums], axis=0)
    v_sum = jnp.concatenate([s[per : 2 * per, :] for s in sums], axis=0)

    def score(keys):
        return lax.dot_general(q, keys, nt, preferred_element_type=jnp.float32) * SCALE2

    row = lax.broadcasted_iota(jnp.int32, (BLOCK, BLOCK), 0)
    col = lax.broadcasted_iota(jnp.int32, (BLOCK, BLOCK), 1)
    s_prev = jnp.where((col > row) | (col >= info_ref[0]), score(kp_ref[...]), NEG)
    s_own = jnp.where(col <= row, score(k_ref[...]), NEG)
    s_sum = jnp.where(bias_ref[...] >= 0.0, score(k_sum), NEG)
    top = jnp.maximum(
        jnp.maximum(jnp.max(s_prev, axis=1, keepdims=True), jnp.max(s_own, axis=1, keepdims=True)),
        jnp.max(s_sum, axis=1, keepdims=True),
    )
    total = jnp.zeros((BLOCK, 1), jnp.float32)
    mixed = jnp.zeros((BLOCK, HD), jnp.float32)
    for s, vals in ((s_prev, vp_ref[...]), (s_own, v_ref[...]), (s_sum, v_sum)):
        e = jnp.exp2(s - top)
        total = total + jnp.sum(e, axis=1, keepdims=True)
        mixed = mixed + jnp.dot(e.astype(jnp.bfloat16), vals, preferred_element_type=jnp.float32)
    out_ref[...] = (mixed / total).astype(jnp.bfloat16)


def attend(block, info, bias, queries, keys, values, prev_k, prev_v, prev_block, sums):
    width = queries.shape[1]
    heads = width // HD
    own = pl.BlockSpec((BLOCK, HD), lambda h: (block, h))
    prev = pl.BlockSpec((BLOCK, HD), lambda h: (prev_block, h))
    sum_rows = sums[0].shape[0]
    piece = pl.BlockSpec((sum_rows, HD), lambda h: (0, h))
    n_keys = 2 * BLOCK + bias.shape[1]
    return pl.pallas_call(
        functools.partial(attend_kernel, len(sums)),
        grid=(heads,),
        in_specs=[
            pl.BlockSpec(memory_space=pltpu.SMEM),
            own,
            prev,
            prev,
            own,
            own,
            pl.BlockSpec((1, bias.shape[1]), lambda h: (0, 0)),
        ]
        + [piece] * len(sums),
        out_specs=pl.BlockSpec((BLOCK, HD), lambda h: (0, h)),
        out_shape=jax.ShapeDtypeStruct((BLOCK, width), jnp.bfloat16),
        compiler_params=pltpu.CompilerParams(vmem_limit_bytes=48 * 1024 * 1024),
        cost_estimate=pl.CostEstimate(
            flops=heads * BLOCK * n_keys * HD * 4,
            bytes_accessed=4 * width * (2 * BLOCK + bias.shape[1]),
            transcendentals=heads * BLOCK * n_keys,
        ),
    )(info, queries, prev_k, prev_v, keys, values, bias, *sums)


def gather_sums(own, count):
    me = lax.axis_index("ctx")
    if count != 16:
        rows = own.shape[0]
        whole = lax.all_gather(own, "ctx", axis=0, tiled=True)
        return [whole[i * rows : (i + 1) * rows] for i in range(count)], [jnp.int32(i) for i in range(count)]

    def up(value, steps):
        return lax.ppermute(value, "ctx", [(i, i + steps) for i in range(count - steps)])

    def flip(value, bit):
        return lax.ppermute(value, "ctx", [(i, i ^ bit) for i in range(count)])

    pieces = [own] + [up(own, 4 * k) for k in (1, 2, 3)]
    source = [me - 4 * k for k in range(4)]
    for bit in (2, 1):
        pieces = pieces + [flip(p, bit) for p in pieces]
        near = jnp.where((me & bit) != 0, -bit, bit)
        source = source + [s + near for s in source]
    return pieces, source


def per_device(n_ctx, n_head, queries, keys, values, w_out):
    rows, width = queries.shape
    blocks = rows // BLOCK
    me = lax.axis_index("ctx")
    side = lax.axis_index("head")
    ends = [slice(b * BLOCK + BLOCK - SUMS, (b + 1) * BLOCK) for b in range(blocks)]
    own = jnp.concatenate([keys[e] for e in ends] + [values[e] for e in ends], axis=0)
    sums, source = gather_sums(own, n_ctx)

    tail = jnp.concatenate([keys[rows - BLOCK :], values[rows - BLOCK :]], axis=0)
    tail, held = lax.optimization_barrier((tail, sums[len(sums) // 2 - 1]))
    sums[len(sums) // 2 - 1] = held
    rim = lax.ppermute(tail, "ctx", [(i, i + 1) for i in range(n_ctx - 1)])

    source_block = (
        jnp.stack(source)[:, None, None] * blocks + jnp.arange(blocks, dtype=jnp.int32)[None, :, None]
    )
    source_block = jnp.broadcast_to(source_block, (len(source), blocks, SUMS)).reshape(1, -1)
    present = source_block >= 0

    out_width = w_out.shape[1] // n_head
    out_parts = [None] * blocks
    for b in list(range(1, blocks)) + [0]:
        bias = jnp.where(present & (source_block <= me * blocks + b - 2), 0.0, NEG).astype(jnp.float32)
        if b == 0:
            info = jnp.where(me == 0, BLOCK, BLOCK - SUMS).astype(jnp.int32).reshape(1)
            att = attend(0, info, bias, queries, keys, values, rim[:BLOCK], rim[BLOCK:], 0, sums)
        else:
            info = jnp.full((1,), BLOCK - SUMS, jnp.int32)
            att = attend(b, info, bias, queries, keys, values, keys, values, b - 1, sums)

        def partial(step):
            at = lax.rem(side + step, n_head) * out_width
            w = lax.dynamic_slice_in_dim(w_out, at, out_width, 1)
            return jnp.dot(att, w, preferred_element_type=jnp.float32).astype(jnp.bfloat16)

        got = [
            lax.ppermute(partial(step), "head", [(i, (i + step) % n_head) for i in range(n_head)])
            for step in range(1, n_head)
        ]
        total = partial(0).astype(jnp.float32)
        for g in got:
            total = total + g.astype(jnp.float32)
        out_parts[b] = total.astype(jnp.bfloat16)
    return jnp.concatenate(out_parts, axis=0)


def solution(mesh):
    in_specs = (P("ctx", "head"), P("ctx", "head"), P("ctx", "head"), P("head", None))
    return jax.shard_map(
        functools.partial(per_device, mesh.shape["ctx"], mesh.shape["head"]),
        mesh=mesh,
        in_specs=in_specs,
        out_specs=P("ctx", "head"),
        check_vma=False,
    )
```

time: 225 us -> 91.3 us (0.41)
  the two profiles are of different devices: /device:TPU:26 before, /device:TPU:0 now
where the time goes in v1:
time: 91.3 us; the launch traced here: 90.2 us
  Pallas kernels  26.3 us (29%)
  starting transfers between devices  23 us (25%)
  waiting for transfers between devices  16.9 us (19%)
  local copies, waits for them, and re-layouts  15.1 us (17%)
  matrix products  4.46 us (5%)
  other arithmetic  4.18 us (5%)
    pallas_call x3, Pallas kernels, attend(): pl.pallas_call(functools.partial(attend_kernel, len(sums)), grid=(heads,)...  26.3 us
    ppermute x3, waiting for transfers between devices, per_device(): lax.ppermute(partial(step), 'head', [(i, (i + step) % n_head) for i in ra...  11.4 us
    ppermute x3, starting transfers between devices, up(): lax.ppermute(value, 'ctx', [(i, i + steps) for i in range(count - steps)])  10.7 us
    ppermute x12, starting transfers between devices, flip(): return lax.ppermute(value, 'ctx', [(i, i ^ bit) for i in range(count)])  5.89 us
    dot_general x6, matrix products, partial(): jnp.dot(att, w, preferred_element_type=jnp.float32).astype(jnp.bfloat16)  4.46 us
    slice x2, local copies, waits for them, and re-layouts, per_device(): tail = jnp.concatenate([keys[rows - BLOCK:], values[rows - BLOCK:]], axis=0)  3.87 us
    unnamed x9, local copies, waits for them, and re-layouts  3.81 us
    ppermute x3, starting transfers between devices, per_device(): lax.ppermute(partial(step), 'head', [(i, (i + step) % n_head) for i in ra...  3.7 us
  transfers between devices with their start and end apart: 19, of which 6 were waited for; matrix products, arithmetic and copies ran while one was open for 19% of the time, Pallas kernels for 29%

profile of v1, /device:TPU:0, one launch (start us, length us, event | category | flops | bytes accessed | tf_op | source)
XLA Modules:
  0.0 90.2 jit_solution(3171347363455921362)
XLA Ops:
  0.0 0.8 slice_dynamic-update-slice_fusion.5
  0.8 0.8 slice_dynamic-update-slice_fusion.4
  1.5 0.8 slice_dynamic-update-slice_fusion.3
  2.3 0.8 slice_dynamic-update-slice_fusion.2
  3.0 0.8 slice_dynamic-update-slice_fusion.1
  3.8 0.8 slice_dynamic-update-slice_fusion.rest_0_
  4.6 7.0 %collective-permute-start = (bf16[96,1024]{1,0:T(8,128)(2,1)S(1)}, bf16[96,1024]{1,0:T(8,128)(2,1)S(1)}, u32[]{:S(2)}, u32[]{:S(2)}) collective-permute-start(bf16[96,1024]{1,0:T(8,128)(2,1)S(1)} %slice_dynamic-update-slice_fusion.rest_0_), channel_id=1, source_target_pairs={{0,24},{2,26},{4,28},{6,30},{1,25},{3,27},{5,29},{7,31}} | collective-permute-start | bytes 589832 | tf_op jit(solution)/shard_map/ppermute | solution.py:87
  11.5 1.3 %collective-permute-start.3 = (bf16[96,1024]{1,0:T(8,128)(2,1)S(1)}, bf16[96,1024]{1,0:T(8,128)(2,1)S(1)}, u32[]{:S(2)}, u32[]{:S(2)}) collective-permute-start(bf16[96,1024]{1,0:T(8,128)(2,1)S(1)} %slice_dynamic-update-slice_fusion.rest_0_), channel_id=1, source_target_pairs={{0,8},{2,10},{4,12},{6,14},{8,16},{10,18},{12,20},{14,22},{16,24},... | collective-permute-start | bytes 589832 | tf_op jit(solution)/shard_map/ppermute | solution.py:87
  12.8 2.5 %collective-permute-start.4 = (bf16[96,1024]{1,0:T(8,128)(2,1)S(1)}, bf16[96,1024]{1,0:T(8,128)(2,1)S(1)}, u32[]{:S(2)}, u32[]{:S(2)}) collective-permute-start(bf16[96,1024]{1,0:T(8,128)(2,1)S(1)} %slice_dynamic-update-slice_fusion.rest_0_), channel_id=1, source_target_pairs={{0,16},{2,18},{4,20},{6,22},{8,24},{10,26},{12,28},{14,30},{1,17},... | collective-permute-start | bytes 589832 | tf_op jit(solution)/shard_map/ppermute | solution.py:87
  15.3 1.5 %collective-permute-done.rest_3_ = bf16[96,1024]{1,0:T(8,128)(2,1)S(1)} collective-permute-done((bf16[96,1024]{1,0:T(8,128)(2,1)S(1)}, bf16[96,1024]{1,0:T(8,128)(2,1)S(1)}, u32[]{:S(2)}, u32[]{:S(2)}) %collective-permute-start) | collective-permute-done | bytes 196640 | tf_op jit(solution)/shard_map/ppermute | solution.py:87
  16.8 1.5 %collective-permute-start.1 = (bf16[96,1024]{1,0:T(8,128)(2,1)S(1)}, bf16[96,1024]{1,0:T(8,128)(2,1)S(1)}, u32[]{:S(2)}, u32[]{:S(2)}) collective-permute-start(bf16[96,1024]{1,0:T(8,128)(2,1)S(1)} %collective-permute-done.rest_3_), channel_id=1, source_target_pairs={{0,4},{2,6},{4,0},{6,2},{8,12},{10,14},{12,8},{14,10},{16,20},{18,... | collective-permute-start | bytes 589832 | tf_op jit(solution)/shard_map/ppermute | solution.py:90
  18.3 0.5 collective-permute-start.5
  18.8 0.0 collective-permute-start.8
  18.8 2.2 %collective-permute-done.3.rest_1_ = bf16[96,1024]{1,0:T(8,128)(2,1)S(1)} collective-permute-done((bf16[96,1024]{1,0:T(8,128)(2,1)S(1)}, bf16[96,1024]{1,0:T(8,128)(2,1)S(1)}, u32[]{:S(2)}, u32[]{:S(2)}) %collective-permute-start.3) | collective-permute-done | bytes 196640 | tf_op jit(solution)/shard_map/ppermute | solution.py:87
  21.0 1.5 %collective-permute-start.6 = (bf16[96,1024]{1,0:T(8,128)(2,1)S(1)}, bf16[96,1024]{1,0:T(8,128)(2,1)S(1)}, u32[]{:S(2)}, u32[]{:S(2)}) collective-permute-start(bf16[96,1024]{1,0:T(8,128)(2,1)S(1)} %collective-permute-done.3.rest_1_), channel_id=1, source_target_pairs={{0,4},{2,6},{4,0},{6,2},{8,12},{10,14},{12,8},{14,10},{16,20},{18,... | collective-permute-start | bytes 589832 | tf_op jit(solution)/shard_map/ppermute | solution.py:90
  22.5 2.0 %slice.30 = bf16[256,1024]{1,0:T(8,128)(2,1)} slice(bf16[768,1024]{1,0:T(8,128)(2,1)} %k_ref.5), slice={[512:768], [0:1024]} | slice | bytes 1048576 | tf_op jit(solution)/shard_map/slice | solution.py:110
  24.5 1.9 %slice.31 = bf16[256,1024]{1,0:T(8,128)(2,1)} slice(bf16[768,1024]{1,0:T(8,128)(2,1)} %v_ref.5), slice={[512:768], [0:1024]} | slice | bytes 1048576 | tf_op jit(solution)/shard_map/slice | solution.py:110
  26.4 0.1 stack.67
  26.5 2.2 %pad_maximum_fusion.1 = bf16[512,1024]{1,0:T(8,128)(2,1)} fusion(bf16[256,1024]{1,0:T(8,128)(2,1)} %slice.31, bf16[256,1024]{1,0:T(8,128)(2,1)} %slice.30), kind=kLoop, calls=%fused_computation.28 | loop fusion | flops 2097152 | bytes 2097152 | tf_op jit(solution)/shard_map/concatenate | solution.py:110
  28.8 0.0 collective-permute-done.4.rest_2_
  28.8 0.5 collective-permute-start.7
  29.3 0.0 collective-permute-done.1.rest_7_
  29.3 0.0 collective-permute-start.10
  29.3 0.0 collective-permute-done.5.rest_4_
  29.3 0.5 collective-permute-start.11
  29.8 0.0 collective-permute-done.8.rest_8_
  29.8 0.1 collective-permute-start.9
  29.9 0.6 collective-permute-done.6.rest_5_
  30.5 2.7 %collective-permute-start.2 = (bf16[512,1024]{1,0:T(8,128)(2,1)}, bf16[512,1024]{1,0:T(8,128)(2,1)}, u32[]{:S(2)}, u32[]{:S(2)}) collective-permute-start(bf16[512,1024]{1,0:T(8,128)(2,1)} %pad_maximum_fusion.1), channel_id=1, source_target_pairs={{0,2},{2,4},{4,6},{6,8},{8,10},{10,12},{12,14},{14,16},{16,18},{18... | collective-permute-start | bytes 3145736 | tf_op jit(solution)/shard_map/ppermute | solution.py:113
  33.2 1.2 %collective-permute-done.7.rest_6_ = bf16[96,1024]{1,0:T(8,128)(2,1)S(1)} collective-permute-done((bf16[96,1024]{1,0:T(8,128)(2,1)S(1)}, bf16[96,1024]{1,0:T(8,128)(2,1)S(1)}, u32[]{:S(2)}, u32[]{:S(2)}) %collective-permute-start.7) | collective-permute-done | bytes 196640 | tf_op jit(solution)/shard_map/ppermute | solution.py:90
  34.4 0.7 collective-permute-start.12
  35.1 0.0 collective-permute-done.10.rest_10_
  35.1 0.1 collective-permute-start.15
  35.2 0.0 collective-permute-done.11.rest_11_
  35.2 0.4 collective-permute-start.13
  35.6 0.0 collective-permute-done.9.rest_9_
  35.6 0.1 collective-permute-start.14
  35.7 0.7 fusion.64
  36.4 0.7 broadcast_in_dim.25
  37.0 0.8 select_n.40.bias_ref
  37.9 0.7 broadcast_in_dim.26
  38.6 0.8 select_n.44.bias_ref
  39.4 1.4 %broadcast_in_dim.27 = f32[16,3,16]{2,1,0:T(4,128)} broadcast(f32[16,3]{1,0:T(8,128)} %get-tuple-element.13), dimensions={0,1} | broadcast | bytes 3264 | tf_op jit(solution)/shard_map/broadcast_in_dim | solution.py:118
  40.8 0.8 select_n.46.bias_ref
  41.7 0.0 collective-permute-done.12.rest_12_
  41.7 0.0 collective-permute-done.14.rest_14_
  41.7 8.8 %shard_map.47 = bf16[256,1024]{1,0:T(8,128)(2,1)S(1)} custom-call(s32[1]{0:T(128)} %constant.53.clone.1.info_ref, bf16[768,1024]{1,0:T(8,128)(2,1)S(1)} %copy-done, bf16[768,1024]{1,0:T(8,128)(2,1)} %k_ref.5, bf16[768,1024]{1,0:T(8,128)(2,1)} %v_ref.5, bf16[768,1024]{1,0:T(8,128)(2,1)} %k_ref.5, bf16[768,1024]{1,0:T(8,128)(2,1)} %v_ref.5, ...), custom_call_target="tpu_custom_call" | custom-call | flops 1342177280 | bytes 5242880 | tf_op jit(solution)/shard_map/pallas_call | solution.py:55
  50.6 0.7 fusion.24
  51.3 1.5 %collective-permute-start.17 = (bf16[256,1024]{1,0:T(8,128)(2,1)S(1)}, bf16[256,1024]{1,0:T(8,128)(2,1)S(1)}, u32[]{:S(2)}, u32[]{:S(2)}) collective-permute-start(bf16[256,1024]{1,0:T(8,128)(2,1)S(1)} %fusion.24), channel_id=1, source_target_pairs={{0,1},{1,0},{2,3},{3,2},{4,5},{5,4},{6,7},{7,6},{8,9},{9,8},{10,11... | collective-permute-start | bytes 1572872 | tf_op jit(solution)/shard_map/ppermute | solution.py:138
  52.9 8.7 %shard_map.48 = bf16[256,1024]{1,0:T(8,128)(2,1)S(1)} custom-call(s32[1]{0:T(128)} %constant.53.clone.1.info_ref, bf16[768,1024]{1,0:T(8,128)(2,1)S(1)} %copy-done, bf16[768,1024]{1,0:T(8,128)(2,1)} %k_ref.5, bf16[768,1024]{1,0:T(8,128)(2,1)} %v_ref.5, bf16[768,1024]{1,0:T(8,128)(2,1)} %k_ref.5, bf16[768,1024]{1,0:T(8,128)(2,1)} %v_ref.5, ...), custom_call_target="tpu_custom_call" | custom-call | flops 1342177280 | bytes 5242880 | tf_op jit(solution)/shard_map/pallas_call | solution.py:55
  61.5 0.7 fusion.27
  62.3 0.6 collective-permute-start.18
  62.9 0.0 collective-permute-done.2
  62.9 1.3 %fusion.73 = (bf16[256,1024]{1,0:T(8,128)(2,1)S(1)}, bf16[256,1024]{1,0:T(8,128)(2,1)S(1)}) fusion(bf16[512,1024]{1,0:T(8,128)(2,1)} %collective-permute-done.2), kind=kLoop, calls=%fused_computation.53 | loop fusion | bytes 2097152 | tf_op jit(solution)/shard_map/slice | solution.py:127
  64.2 8.8 %shard_map.46 = bf16[256,1024]{1,0:T(8,128)(2,1)S(1)} custom-call(s32[1]{0:T(128)} %bitcast.info_ref, bf16[768,1024]{1,0:T(8,128)(2,1)} %q_ref.5, bf16[256,1024]{1,0:T(8,128)(2,1)S(1)} %get-tuple-element.10.kp_ref, bf16[256,1024]{1,0:T(8,128)(2,1)S(1)} %get-tuple-element.9.vp_ref, bf16[768,1024]{1,0:T(8,128)(2,1)} %k_ref.5, bf16[768,1024]{1,0:T(8,128)(2,1)} %v_ref.5, ...), custom_call_target="tpu_custom_call" | custom-call | flops 1342177280 | bytes 5242880 | tf_op jit(solution)/shard_map/pallas_call | solution.py:55
  73.0 0.7 fusion.21
  73.7 1.5 %collective-permute-start.16 = (bf16[256,1024]{1,0:T(8,128)(2,1)S(1)}, bf16[256,1024]{1,0:T(8,128)(2,1)S(1)}, u32[]{:S(2)}, u32[]{:S(2)}) collective-permute-start(bf16[256,1024]{1,0:T(8,128)(2,1)S(1)} %fusion.21), channel_id=1, source_target_pairs={{0,1},{1,0},{2,3},{3,2},{4,5},{5,4},{6,7},{7,6},{8,9},{9,8},{10,11... | collective-permute-start | bytes 1572872 | tf_op jit(solution)/shard_map/ppermute | solution.py:138
  75.3 0.0 collective-permute-done.17
  75.3 0.7 fusion.45
  76.0 1.4 %collective-permute-done.18 = bf16[256,1024]{1,0:T(8,128)(2,1)S(1)} collective-permute-done((bf16[256,1024]{1,0:T(8,128)(2,1)S(1)}, bf16[256,1024]{1,0:T(8,128)(2,1)S(1)}, u32[]{:S(2)}, u32[]{:S(2)}) %collective-permute-start.18) | collective-permute-done | bytes 524320 | tf_op jit(solution)/shard_map/ppermute | solution.py:138
  77.4 0.7 fusion.36
  78.1 10.0 %collective-permute-done.16 = bf16[256,1024]{1,0:T(8,128)(2,1)S(1)} collective-permute-done((bf16[256,1024]{1,0:T(8,128)(2,1)S(1)}, bf16[256,1024]{1,0:T(8,128)(2,1)S(1)}, u32[]{:S(2)}, u32[]{:S(2)}) %collective-permute-start.16) | collective-permute-done | bytes 524320 | tf_op jit(solution)/shard_map/ppermute | solution.py:138
  88.1 0.7 fusion.54
  88.9 1.3 %pad_maximum_fusion = bf16[768,1024]{1,0:T(8,128)(2,1)} fusion(bf16[256,1024]{1,0:T(8,128)(2,1)S(1)} %fusion.36, bf16[256,1024]{1,0:T(8,128)(2,1)S(1)} %fusion.45, bf16[256,1024]{1,0:T(8,128)(2,1)S(1)} %fusion.54), kind=kLoop, calls=%fused_computation.12 | loop fusion | flops 4718592 | bytes 3145728 | tf_op jit(solution)/shard_map/concatenate | solution.py:145
  (7 shorter events, 0.0 us)
Async XLA Ops:
  4.6 12.2 %collective-permute-start = (bf16[96,1024]{1,0:T(8,128)(2,1)S(1)}, bf16[96,1024]{1,0:T(8,128)(2,1)S(1)}, u32[]{:S(2)}, u32[]{:S(2)}) collective-permute-start(bf16[96,1024]{1,0:T(8,128)(2,1)S(1)} %slice_dynamic-update-slice_fusion.rest_0_), channel_id=1, source_target_pairs={{0,24},{2,26},{4,28},{6,30},{1,25},{3,27},{5,29},{7,31}} | collective-permute-start | bytes 589832 | tf_op jit(solution)/shard_map/ppermute | solution.py:87
  11.5 9.5 %collective-permute-start.3 = (bf16[96,1024]{1,0:T(8,128)(2,1)S(1)}, bf16[96,1024]{1,0:T(8,128)(2,1)S(1)}, u32[]{:S(2)}, u32[]{:S(2)}) collective-permute-start(bf16[96,1024]{1,0:T(8,128)(2,1)S(1)} %slice_dynamic-update-slice_fusion.rest_0_), channel_id=1, source_target_pairs={{0,8},{2,10},{4,12},{6,14},{8,16},{10,18},{12,20},{14,22},{16,24},... | collective-permute-start | bytes 589832 | tf_op jit(solution)/shard_map/ppermute | solution.py:87
  12.8 15.9 %collective-permute-start.4 = (bf16[96,1024]{1,0:T(8,128)(2,1)S(1)}, bf16[96,1024]{1,0:T(8,128)(2,1)S(1)}, u32[]{:S(2)}, u32[]{:S(2)}) collective-permute-start(bf16[96,1024]{1,0:T(8,128)(2,1)S(1)} %slice_dynamic-update-slice_fusion.rest_0_), channel_id=1, source_target_pairs={{0,16},{2,18},{4,20},{6,22},{8,24},{10,26},{12,28},{14,30},{1,17},... | collective-permute-start | bytes 589832 | tf_op jit(solution)/shard_map/ppermute | solution.py:87
  16.8 12.5 %collective-permute-start.1 = (bf16[96,1024]{1,0:T(8,128)(2,1)S(1)}, bf16[96,1024]{1,0:T(8,128)(2,1)S(1)}, u32[]{:S(2)}, u32[]{:S(2)}) collective-permute-start(bf16[96,1024]{1,0:T(8,128)(2,1)S(1)} %collective-permute-done.rest_3_), channel_id=1, source_target_pairs={{0,4},{2,6},{4,0},{6,2},{8,12},{10,14},{12,8},{14,10},{16,20},{18,... | collective-permute-start | bytes 589832 | tf_op jit(solution)/shard_map/ppermute | solution.py:90
  18.3 10.9 %collective-permute-start.5 = (bf16[96,1024]{1,0:T(8,128)(2,1)S(1)}, bf16[96,1024]{1,0:T(8,128)(2,1)S(1)}, u32[]{:S(2)}, u32[]{:S(2)}) collective-permute-start(bf16[96,1024]{1,0:T(8,128)(2,1)S(1)} %slice_dynamic-update-slice_fusion.rest_0_), channel_id=1, source_target_pairs={{0,4},{2,6},{4,0},{6,2},{8,12},{10,14},{12,8},{14,10},{16,20},{18,... | collective-permute-start | bytes 589832 | tf_op jit(solution)/shard_map/ppermute | solution.py:90
  18.8 10.9 %collective-permute-start.8 = (bf16[96,1024]{1,0:T(8,128)(2,1)S(1)}, bf16[96,1024]{1,0:T(8,128)(2,1)S(1)}, u32[]{:S(2)}, u32[]{:S(2)}) collective-permute-start(bf16[96,1024]{1,0:T(8,128)(2,1)S(1)} %slice_dynamic-update-slice_fusion.rest_0_), channel_id=1, source_target_pairs={{0,2},{2,0},{4,6},{6,4},{8,10},{10,8},{12,14},{14,12},{16,18},{18,... | collective-permute-start | bytes 589832 | tf_op jit(solution)/shard_map/ppermute | solution.py:90
  21.0 9.5 %collective-permute-start.6 = (bf16[96,1024]{1,0:T(8,128)(2,1)S(1)}, bf16[96,1024]{1,0:T(8,128)(2,1)S(1)}, u32[]{:S(2)}, u32[]{:S(2)}) collective-permute-start(bf16[96,1024]{1,0:T(8,128)(2,1)S(1)} %collective-permute-done.3.rest_1_), channel_id=1, source_target_pairs={{0,4},{2,6},{4,0},{6,2},{8,12},{10,14},{12,8},{14,10},{16,20},{18,... | collective-permute-start | bytes 589832 | tf_op jit(solution)/shard_map/ppermute | solution.py:90
  22.5 19.2 %copy-start = (bf16[768,1024]{1,0:T(8,128)(2,1)S(1)}, bf16[768,1024]{1,0:T(8,128)(2,1)}, u32[]{:S(2)}) copy-start(bf16[768,1024]{1,0:T(8,128)(2,1)} %q_ref.5) | copy-start | bytes 4718596
  28.8 5.7 %collective-permute-start.7 = (bf16[96,1024]{1,0:T(8,128)(2,1)S(1)}, bf16[96,1024]{1,0:T(8,128)(2,1)S(1)}, u32[]{:S(2)}, u32[]{:S(2)}) collective-permute-start(bf16[96,1024]{1,0:T(8,128)(2,1)S(1)} %collective-permute-done.4.rest_2_), channel_id=1, source_target_pairs={{0,4},{2,6},{4,0},{6,2},{8,12},{10,14},{12,8},{14,10},{16,20},{18,... | collective-permute-start | bytes 589832 | tf_op jit(solution)/shard_map/ppermute | solution.py:90
  29.3 5.8 %collective-permute-start.10 = (bf16[96,1024]{1,0:T(8,128)(2,1)S(1)}, bf16[96,1024]{1,0:T(8,128)(2,1)S(1)}, u32[]{:S(2)}, u32[]{:S(2)}) collective-permute-start(bf16[96,1024]{1,0:T(8,128)(2,1)S(1)} %collective-permute-done.4.rest_2_), channel_id=1, source_target_pairs={{0,2},{2,0},{4,6},{6,4},{8,10},{10,8},{12,14},{14,12},{16,18},{18,... | collective-permute-start | bytes 589832 | tf_op jit(solution)/shard_map/ppermute | solution.py:90
  29.3 5.9 %collective-permute-start.11 = (bf16[96,1024]{1,0:T(8,128)(2,1)S(1)}, bf16[96,1024]{1,0:T(8,128)(2,1)}, u32[]{:S(2)}, u32[]{:S(2)}) collective-permute-start(bf16[96,1024]{1,0:T(8,128)(2,1)S(1)} %collective-permute-done.rest_3_), channel_id=1, source_target_pairs={{0,2},{2,0},{4,6},{6,4},{8,10},{10,8},{12,14},{14,12},{16,18},{18,... | collective-permute-start | bytes 589832 | tf_op jit(solution)/shard_map/ppermute | solution.py:90
  29.8 5.8 %collective-permute-start.9 = (bf16[96,1024]{1,0:T(8,128)(2,1)S(1)}, bf16[96,1024]{1,0:T(8,128)(2,1)}, u32[]{:S(2)}, u32[]{:S(2)}) collective-permute-start(bf16[96,1024]{1,0:T(8,128)(2,1)S(1)} %collective-permute-done.3.rest_1_), channel_id=1, source_target_pairs={{0,2},{2,0},{4,6},{6,4},{8,10},{10,8},{12,14},{14,12},{16,18},{18,... | collective-permute-start | bytes 589832 | tf_op jit(solution)/shard_map/ppermute | solution.py:90
  30.5 32.4 %collective-permute-start.2 = (bf16[512,1024]{1,0:T(8,128)(2,1)}, bf16[512,1024]{1,0:T(8,128)(2,1)}, u32[]{:S(2)}, u32[]{:S(2)}) collective-permute-start(bf16[512,1024]{1,0:T(8,128)(2,1)} %pad_maximum_fusion.1), channel_id=1, source_target_pairs={{0,2},{2,4},{4,6},{6,8},{8,10},{10,12},{12,14},{14,16},{16,18},{18... | collective-permute-start | bytes 3145736 | tf_op jit(solution)/shard_map/ppermute | solution.py:113
  34.4 7.3 %collective-permute-start.12 = (bf16[96,1024]{1,0:T(8,128)(2,1)S(1)}, bf16[96,1024]{1,0:T(8,128)(2,1)}, u32[]{:S(2)}, u32[]{:S(2)}) collective-permute-start(bf16[96,1024]{1,0:T(8,128)(2,1)S(1)} %collective-permute-done.5.rest_4_), channel_id=1, source_target_pairs={{0,2},{2,0},{4,6},{6,4},{8,10},{10,8},{12,14},{14,12},{16,18},{18,... | collective-permute-start | bytes 589832 | tf_op jit(solution)/shard_map/ppermute | solution.py:90
  35.1 6.6 %collective-permute-start.15 = (bf16[96,1024]{1,0:T(8,128)(2,1)S(1)}, bf16[96,1024]{1,0:T(8,128)(2,1)}, u32[]{:S(2)}, u32[]{:S(2)}) collective-permute-start(bf16[96,1024]{1,0:T(8,128)(2,1)S(1)} %collective-permute-done.1.rest_7_), channel_id=1, source_target_pairs={{0,2},{2,0},{4,6},{6,4},{8,10},{10,8},{12,14},{14,12},{16,18},{18,... | collective-permute-start | bytes 589832 | tf_op jit(solution)/shard_map/ppermute | solution.py:90
  35.2 6.5 %collective-permute-start.13 = (bf16[96,1024]{1,0:T(8,128)(2,1)S(1)}, bf16[96,1024]{1,0:T(8,128)(2,1)}, u32[]{:S(2)}, u32[]{:S(2)}) collective-permute-start(bf16[96,1024]{1,0:T(8,128)(2,1)S(1)} %collective-permute-done.6.rest_5_), channel_id=1, source_target_pairs={{0,2},{2,0},{4,6},{6,4},{8,10},{10,8},{12,14},{14,12},{16,18},{18,... | collective-permute-start | bytes 589832 | tf_op jit(solution)/shard_map/ppermute | solution.py:90
  35.6 6.1 %collective-permute-start.14 = (bf16[96,1024]{1,0:T(8,128)(2,1)S(1)}, bf16[96,1024]{1,0:T(8,128)(2,1)}, u32[]{:S(2)}, u32[]{:S(2)}) collective-permute-start(bf16[96,1024]{1,0:T(8,128)(2,1)S(1)} %collective-permute-done.7.rest_6_), channel_id=1, source_target_pairs={{0,2},{2,0},{4,6},{6,4},{8,10},{10,8},{12,14},{14,12},{16,18},{18,... | collective-permute-start | bytes 589832 | tf_op jit(solution)/shard_map/ppermute | solution.py:90
  41.7 8.9 %copy-start.1 = (bf16[1024,2048]{1,0:T(8,128)(2,1)S(1)}, bf16[1024,2048]{1,0:T(8,128)(2,1)}, u32[]{:S(2)}) copy-start(bf16[1024,2048]{1,0:T(8,128)(2,1)} %param.7) | copy-start | bytes 12582916
  51.3 23.9 %collective-permute-start.17 = (bf16[256,1024]{1,0:T(8,128)(2,1)S(1)}, bf16[256,1024]{1,0:T(8,128)(2,1)S(1)}, u32[]{:S(2)}, u32[]{:S(2)}) collective-permute-start(bf16[256,1024]{1,0:T(8,128)(2,1)S(1)} %fusion.24), channel_id=1, source_target_pairs={{0,1},{1,0},{2,3},{3,2},{4,5},{5,4},{6,7},{7,6},{8,9},{9,8},{10,11... | collective-permute-start | bytes 1572872 | tf_op jit(solution)/shard_map/ppermute | solution.py:138
  62.3 15.1 %collective-permute-start.18 = (bf16[256,1024]{1,0:T(8,128)(2,1)S(1)}, bf16[256,1024]{1,0:T(8,128)(2,1)S(1)}, u32[]{:S(2)}, u32[]{:S(2)}) collective-permute-start(bf16[256,1024]{1,0:T(8,128)(2,1)S(1)} %fusion.27), channel_id=1, source_target_pairs={{0,1},{1,0},{2,3},{3,2},{4,5},{5,4},{6,7},{7,6},{8,9},{9,8},{10,11... | collective-permute-start | bytes 1572872 | tf_op jit(solution)/shard_map/ppermute | solution.py:138
  73.7 14.4 %collective-permute-start.16 = (bf16[256,1024]{1,0:T(8,128)(2,1)S(1)}, bf16[256,1024]{1,0:T(8,128)(2,1)S(1)}, u32[]{:S(2)}, u32[]{:S(2)}) collective-permute-start(bf16[256,1024]{1,0:T(8,128)(2,1)S(1)} %fusion.21), channel_id=1, source_target_pairs={{0,1},{1,0},{2,3},{3,2},{4,5},{5,4},{6,7},{7,6},{8,9},{9,8},{10,11... | collective-permute-start | bytes 1572872 | tf_op jit(solution)/shard_map/ppermute | solution.py:138

commit v2 on v0

v2 whole, which is shorter than its diff:
```python
import functools
import math

import jax
import jax.numpy as jnp
from jax import lax
from jax.experimental import pallas as pl
from jax.experimental.pallas import tpu as pltpu
from jax.sharding import PartitionSpec as P

HD = 128
BLOCK = 256
SUMS = 16
NEG = -3.3e38
SCALE2 = math.log2(math.e) / math.sqrt(HD)
MIB = 1024 * 1024
GROUP = 4


def copy_rows_kernel(*refs):
    out_ref, at = refs[-1], 0
    for ref in refs[:-1]:
        out_ref[at : at + ref.shape[0], :] = ref[...]
        at += ref.shape[0]


def copy_rows(parts, limit):
    width = parts[0][0].shape[1]
    total = sum(rows for _, rows, _ in parts)
    return pl.pallas_call(
        copy_rows_kernel,
        grid=(1,),
        in_specs=[pl.BlockSpec((rows, width), lambda i, at=at: (at, 0)) for _, rows, at in parts],
        out_specs=pl.BlockSpec((total, width), lambda i: (0, 0)),
        out_shape=jax.ShapeDtypeStruct((total, width), jnp.bfloat16),
        compiler_params=pltpu.CompilerParams(vmem_limit_bytes=limit),
        cost_estimate=pl.CostEstimate(flops=0, bytes_accessed=4 * total * width, transcendentals=0),
    )(*[array for array, _, _ in parts])


def source_of(key, me):
    if isinstance(key, int):
        return jnp.int32(key)
    up, flip_y, flip_core = key
    source = me - 4 * up
    for bit, flipped in ((2, flip_y), (1, flip_core)):
        if flipped:
            source = source + jnp.where((me & bit) != 0, -bit, bit)
    return source


def attend_kernel(cfg, *refs):
    blocks, block, first, keys_of, band, carried, finish = cfg
    refs = list(refs)
    q_ref = refs.pop(0)
    band_refs = [refs.pop(0) for _ in range(4 if band else 0)]
    sums = [refs.pop(0) for _ in keys_of]
    state = [refs.pop(0) for _ in range(2 if carried else 0)]
    rows, width = q_ref.shape
    me = lax.axis_index("ctx")
    if finish:
        (out_ref,) = refs
    else:
        acc_ref, stat_ref = refs

    per = sums[0].shape[0] // 2
    n_sum = len(sums) * per
    sum_col = lax.broadcasted_iota(jnp.int32, (1, n_sum), 1)
    end = jnp.zeros((1, n_sum), jnp.int32)
    for i, key in enumerate(keys_of):
        source = source_of(key, me)
        count = jnp.clip(SUMS * (blocks * (me - source) + block - 1), 0, per)
        count = jnp.where(source < 0, 0, count)
        end = jnp.where(sum_col >= i * per, i * per + count, end)
    allowed = [sum_col < end]
    if band:
        row = first + lax.broadcasted_iota(jnp.int32, (rows, BLOCK), 0)
        col = lax.broadcasted_iota(jnp.int32, (rows, BLOCK), 1)
        tail = BLOCK - SUMS
        if block == 0:
            tail = jnp.where(me == 0, BLOCK, tail)
        low, high = first // HD * HD, first + rows
        allowed = [((col > row) | (col >= tail))[:, low:], (col <= row)[:, :high]] + allowed
        cuts = [slice(low, BLOCK), slice(0, high)]
    else:
        cuts = []
    nt = (((1,), (1,)), ((), ()))
    lane = lax.broadcasted_iota(jnp.int32, (rows, HD), 1)
    stats = jnp.zeros((rows, HD), jnp.float32)

    for j in range(width // HD):
        c = slice(j * HD, (j + 1) * HD)
        q = q_ref[:, c]
        keys = [r[cut, c] for r, cut in zip(band_refs[0::2], cuts)] + [jnp.concatenate([s[0:per, c] for s in sums], axis=0)]
        vals = [r[cut, c] for r, cut in zip(band_refs[1::2], cuts)] + [s[per : 2 * per, c] for s in sums]
        score = jnp.concatenate(
            [
                jnp.where(ok, lax.dot_general(q, k, nt, preferred_element_type=jnp.float32) * SCALE2, NEG)
                for ok, k in zip(allowed, keys)
            ],
            axis=1,
        )
        top = jnp.max(score, axis=1, keepdims=True)
        if carried:
            old_top, old_total = state[1][:, j : j + 1], state[1][:, 8 + j : 9 + j]
            top = jnp.maximum(top, old_top)
        weight = jnp.exp2(score - top).astype(jnp.bfloat16)
        vals = jnp.concatenate(vals, axis=0)
        vals = jnp.concatenate([vals, jnp.ones_like(vals)], axis=1)
        mixed = jnp.dot(weight, vals, preferred_element_type=jnp.float32)
        mixed, total = mixed[:, :HD], mixed[:, HD:]
        if carried:
            keep = jnp.exp2(old_top - top)
            mixed = mixed + keep * state[0][:, c]
            total = total + keep * old_total
        if finish:
            out_ref[:, c] = (mixed / total).astype(jnp.bfloat16)
        else:
            acc_ref[:, c] = mixed
            stats = jnp.where(lane == j, top, jnp.where(lane == 8 + j, total, stats))
    if not finish:
        stat_ref[...] = stats


def attend(block, first, rows, queries, pieces, band=None, state=None, finish=True):
    width = queries.shape[1]
    part = min(width, GROUP * HD)
    steps = width // part
    blocks = queries.shape[0] // BLOCK
    at_row = (block * BLOCK + first) // rows
    operands, specs = [queries], [pl.BlockSpec((rows, part), lambda h: (at_row, h))]
    for array, at in band or []:
        operands.append(array)
        specs.append(pl.BlockSpec((BLOCK, part), lambda h, at=at: (at, h)))
    for piece in pieces.values():
        operands.append(piece)
        specs.append(pl.BlockSpec((piece.shape[0], part), lambda h: (0, h)))
    acc_spec = pl.BlockSpec((rows, part), lambda h: (0, h))
    stat_spec = pl.BlockSpec((rows, HD), lambda h: (0, h))
    if state is not None:
        operands += state
        specs += [acc_spec, stat_spec]
    if finish:
        out_specs = acc_spec
        out_shape = jax.ShapeDtypeStruct((rows, width), jnp.bfloat16)
    else:
        out_specs = [acc_spec, stat_spec]
        out_shape = [jax.ShapeDtypeStruct((rows, n), jnp.float32) for n in (width, steps * HD)]
    n_keys = (2 * BLOCK if band else 0) + sum(p.shape[0] for p in pieces.values()) // 2
    cfg = (blocks, block, first, tuple(pieces), band is not None, state is not None, finish)
    return pl.pallas_call(
        functools.partial(attend_kernel, cfg),
        grid=(steps,),
        in_specs=specs,
        out_specs=out_specs,
        out_shape=out_shape,
        compiler_params=pltpu.CompilerParams(vmem_limit_bytes=50 * MIB),
        cost_estimate=pl.CostEstimate(
            flops=width * rows * n_keys * 4,
            bytes_accessed=4 * width * n_keys,
            transcendentals=width // HD * rows * n_keys,
        ),
    )(*operands)


def add_kernel(n_parts, *refs):
    total = refs[0][...].astype(jnp.float32)
    for ref in refs[1:n_parts]:
        total = total + ref[...].astype(jnp.float32)
    refs[-1][...] = total.astype(jnp.bfloat16)


def add_into(out, rows_total, at, parts):
    rows, width = parts[0].shape
    part = pl.BlockSpec((rows, width), lambda i: (0, 0))
    extra = [] if out is None else [out]
    return pl.pallas_call(
        functools.partial(add_kernel, len(parts)),
        grid=(1,),
        in_specs=[part] * len(parts) + [pl.BlockSpec(memory_space=pl.ANY)] * len(extra),
        out_specs=pl.BlockSpec((rows, width), lambda i: (at // rows, 0)),
        out_shape=jax.ShapeDtypeStruct((rows_total, width), jnp.bfloat16),
        input_output_aliases={len(parts): 0} if extra else {},
        compiler_params=pltpu.CompilerParams(vmem_limit_bytes=8 * MIB),
        cost_estimate=pl.CostEstimate(flops=0, bytes_accessed=8 * rows * width, transcendentals=0),
    )(*parts, *extra)


def per_device(n_ctx, n_head, queries, keys, values, w_out):
    rows = queries.shape[0]
    blocks = rows // BLOCK
    side = lax.axis_index("head")
    ends = [BLOCK // SUMS * (b + 1) - 1 for b in range(blocks)]
    own = copy_rows([(a, SUMS, e) for a in (keys, values) for e in ends], 61 * MIB)
    tie = lax.optimization_barrier

    def band_of(b):
        return [(keys, b - 1), (values, b - 1), (keys, b), (values, b)]

    def tail_rows(k, v):
        return copy_rows([(a, BLOCK, blocks - 1) for a in (k, v)], 8 * MIB)

    early = {}
    states = {b: None for b in range(blocks)}
    if n_ctx != 16:
        whole = lax.all_gather(own, "ctx", axis=0, tiled=True)
        size = own.shape[0]
        late = {i: whole[i * size : (i + 1) * size] for i in range(n_ctx)}
        tail = tail_rows(keys, values)
    else:

        def send(value, pairs):
            return lax.ppermute(value, "ctx", pairs)

        def up(value, least):
            return send(value, [(i, i + 4) for i in range(4 * least - 4, n_ctx - 4)])

        def flip(value, bit):
            return send(value, [(i, i ^ bit) for i in range(n_ctx)])

        z1, y0 = up(own, 1), flip(own, 2)
        far = send(own, [(i, (i + 12) ^ 2) for i in range(4)])
        z1, y0 = tie((z1, y0))
        z2, y1 = up(z1, 2), flip(z1, 2)
        z2, y1, tail = tie((z2, y1, tail_rows(keys, values)))
        z3, y2 = up(z2, 3), flip(z2, 2)
        z3, tail = tie((z3, tail))
        early = {(0, 0, 0): own, (1, 0, 0): z1, (0, 1, 0): y0}
        early |= {(k, y, 1): flip(p, 1) for (k, y, _), p in list(early.items())}
        late = {(2, 0, 0): z2, (1, 1, 0): y1, (3, 0, 0): z3, (2, 1, 0): y2, (3, 1, 0): far}
        late |= {(k, y, 1): flip(p, 1) for (k, y, _), p in list(late.items())}

    rim = lax.ppermute(tail, "ctx", [(i, i + 1) for i in range(n_ctx - 1)])
    half = BLOCK // 2
    chunks = [(1, 0, half), (1, half, half)] + [(b, 0, BLOCK) for b in range(2, blocks)] + [(0, 0, BLOCK)]
    sent, kept, parts = [], [], []
    out_width = w_out.shape[1] // n_head
    for b, first, count in chunks:
        if len(parts) > 1:
            queries, parts[-2], _ = tie((queries, parts[-2], sent[-1]))
        elif parts:
            queries, _ = tie((queries, sent[-1]))
        if states[b] is not None:
            att = attend(b, first, count, queries, late, state=states[b])
        else:
            band = band_of(b) if b else [(rim, 0), (rim, 1), (keys, 0), (values, 0)]
            att = attend(b, first, count, queries, early | late, band=band)

        def partial(step):
            at = lax.rem(side + step, n_head) * out_width
            w = lax.dynamic_slice_in_dim(w_out, at, out_width, 1)
            return jnp.dot(att, w, preferred_element_type=jnp.float32).astype(jnp.bfloat16)

        sent.append([partial(step) for step in range(1, n_head)])
        kept.append(partial(0))
        parts.append(
            [
                lax.ppermute(value, "head", [(i, (i + step) % n_head) for i in range(n_head)])
                for step, value in enumerate(sent[-1], 1)
            ]
        )
    kept, _ = tie((kept, sent[-1]))
    out = None
    for (b, first, count), received, own_part in zip(chunks, parts, kept):
        out = add_into(out, rows, b * BLOCK + first, received + [own_part])
    return out


def solution(mesh):
    in_specs = (P("ctx", "head"), P("ctx", "head"), P("ctx", "head"), P("head", None))
    return jax.shard_map(
        functools.partial(per_device, mesh.shape["ctx"], mesh.shape["head"]),
        mesh=mesh,
        in_specs=in_specs,
        out_specs=P("ctx", "head"),
        check_vma=False,
    )
```

time: 225 us -> 84.9 us (0.38)
  the two profiles are of different devices: /device:TPU:26 before, /device:TPU:17 now
where the time goes in v2:
time: 84.9 us; the launch traced here: 84.6 us
  starting transfers between devices  31.2 us (37%)
  Pallas kernels  24.5 us (29%)
  waiting for transfers between devices  20.6 us (24%)
  matrix products  4.67 us (6%)
  local copies, waits for them, and re-layouts  3.35 us (4%)
    ppermute x15, starting transfers between devices, send(): return lax.ppermute(value, 'ctx', pairs)  23.7 us
    pallas_call x4, Pallas kernels, attend(): pl.pallas_call(functools.partial(attend_kernel, cfg), grid=(steps,), in_s...  19.4 us
    ppermute x4, waiting for transfers between devices, per_device(): lax.ppermute(value, 'head', [(i, (i + step) % n_head) for i in range(n_he...  12.3 us
    ppermute x15, waiting for transfers between devices, send(): return lax.ppermute(value, 'ctx', pairs)  8.33 us
    dot_general x8, matrix products, partial(): jnp.dot(att, w, preferred_element_type=jnp.float32).astype(jnp.bfloat16)  4.67 us
    ppermute x1, starting transfers between devices, per_device(): rim = lax.ppermute(tail, 'ctx', [(i, i + 1) for i in range(n_ctx - 1)])  4.01 us
    ppermute x4, starting transfers between devices, per_device(): lax.ppermute(value, 'head', [(i, (i + step) % n_head) for i in range(n_he...  3.53 us
    pallas_call x4, Pallas kernels, add_into(): pl.pallas_call(functools.partial(add_kernel, len(parts)), grid=(1,), in_s...  3.36 us
  transfers between devices with their start and end apart: 20, of which 7 were waited for; matrix products, arithmetic and copies ran while one was open for 6% of the time, Pallas kernels for 26%

profile of v2, /device:TPU:17, one launch (start us, length us, event | category | flops | bytes accessed | tf_op | source)
XLA Modules:
  0.0 84.6 jit_solution(17212072213574615273)
XLA Ops:
  0.0 1.6 %shard_map.46.refs_5_ = bf16[96,1024]{1,0:T(8,128)(2,1)} custom-call(bf16[768,1024]{1,0:T(8,128)(2,1)} %refs_3_.9, bf16[768,1024]{1,0:T(8,128)(2,1)} %refs_3_.9, bf16[768,1024]{1,0:T(8,128)(2,1)} %refs_3_.9, bf16[768,1024]{1,0:T(8,128)(2,1)} %refs_4_.9, bf16[768,1024]{1,0:T(8,128)(2,1)} %refs_4_.9, bf16[768,1024]{1,0:T(8,128)(2,1)} %refs_4_.9), custom_call_target="tpu_custom_call" | custom-call | bytes 393216 | tf_op jit(solution)/shard_map/pallas_call | solution.py:30
  1.6 1.2 %collective-permute-start.1 = (bf16[96,1024]{1,0:T(8,128)(2,1)}, bf16[96,1024]{1,0:T(8,128)(2,1)S(1)}, u32[]{:S(2)}, u32[]{:S(2)}) collective-permute-start(bf16[96,1024]{1,0:T(8,128)(2,1)} %shard_map.46.refs_5_), channel_id=1, source_target_pairs={{0,4},{2,6},{4,0},{6,2},{8,12},{10,14},{12,8},{14,10},{16,20},{18,... | collective-permute-start | bytes 589832 | tf_op jit(solution)/shard_map/ppermute | solution.py:213
  2.9 3.2 %collective-permute-start = (bf16[96,1024]{1,0:T(8,128)(2,1)}, bf16[96,1024]{1,0:T(8,128)(2,1)S(1)}, u32[]{:S(2)}, u32[]{:S(2)}) collective-permute-start(bf16[96,1024]{1,0:T(8,128)(2,1)} %shard_map.46.refs_5_), channel_id=1, source_target_pairs={{0,8},{2,10},{4,12},{6,14},{8,16},{10,18},{12,20},{14,22},{16,24},... | collective-permute-start | bytes 589832 | tf_op jit(solution)/shard_map/ppermute | solution.py:213
  6.1 1.5 %collective-permute-done.1.refs_7_ = bf16[96,1024]{1,0:T(8,128)(2,1)S(1)} collective-permute-done((bf16[96,1024]{1,0:T(8,128)(2,1)}, bf16[96,1024]{1,0:T(8,128)(2,1)S(1)}, u32[]{:S(2)}, u32[]{:S(2)}) %collective-permute-start.1) | collective-permute-done | bytes 196640 | tf_op jit(solution)/shard_map/ppermute | solution.py:213
  7.6 2.8 %collective-permute-done.refs_6_ = bf16[96,1024]{1,0:T(8,128)(2,1)S(1)} collective-permute-done((bf16[96,1024]{1,0:T(8,128)(2,1)}, bf16[96,1024]{1,0:T(8,128)(2,1)S(1)}, u32[]{:S(2)}, u32[]{:S(2)}) %collective-permute-start) | collective-permute-done | bytes 196640 | tf_op jit(solution)/shard_map/ppermute | solution.py:213
  10.4 0.2 collective-permute-start.6
  10.7 3.2 %collective-permute-start.5 = (bf16[96,1024]{1,0:T(8,128)(2,1)S(1)}, bf16[96,1024]{1,0:T(8,128)(2,1)S(1)}, u32[]{:S(2)}, u32[]{:S(2)}) collective-permute-start(bf16[96,1024]{1,0:T(8,128)(2,1)S(1)} %collective-permute-done.refs_6_), channel_id=1, source_target_pairs={{8,16},{10,18},{12,20},{14,22},{16,24},{18,26},{20,28},{22,30},{9,... | collective-permute-start | bytes 589832 | tf_op jit(solution)/shard_map/ppermute | solution.py:213
  13.9 0.7 collective-permute-start.9
  14.6 0.0 copy-start.1
  14.6 1.4 %copy-done.1 = bf16[768,1024]{1,0:T(8,128)(2,1)S(1)} copy-done((bf16[768,1024]{1,0:T(8,128)(2,1)S(1)}, bf16[768,1024]{1,0:T(8,128)(2,1)}, u32[]{:S(2)}) %copy-start.1) | copy-done | bytes 1572888
  16.0 0.1 shard_map.47
  16.0 0.0 copy-start.3
  16.0 1.0 %copy-done.3 = bf16[512,1024]{1,0:T(8,128)(2,1)} copy-done((bf16[512,1024]{1,0:T(8,128)(2,1)}, bf16[512,1024]{1,0:T(8,128)(2,1)S(1)}, u32[]{:S(2)}) %copy-start.3) | copy-done | bytes 1048600
  17.0 0.0 collective-permute-done.6.refs_12_
  17.0 0.3 collective-permute-done.5.refs_11_
  17.4 3.2 %collective-permute-start.7 = (bf16[96,1024]{1,0:T(8,128)(2,1)S(1)}, bf16[96,1024]{1,0:T(8,128)(2,1)S(1)}, u32[]{:S(2)}, u32[]{:S(2)}) collective-permute-start(bf16[96,1024]{1,0:T(8,128)(2,1)S(1)} %collective-permute-done.5.refs_11_), channel_id=1, source_target_pairs={{16,24},{18,26},{20,28},{22,30},{17,25},{19,27},{21,29},{23,31}} | collective-permute-start | bytes 589832 | tf_op jit(solution)/shard_map/ppermute | solution.py:213
  20.6 0.0 copy-done.2
  20.6 5.5 %collective-permute-start.2 = (bf16[96,1024]{1,0:T(8,128)(2,1)S(1)}, bf16[96,1024]{1,0:T(8,128)(2,1)S(1)}, u32[]{:S(2)}, u32[]{:S(2)}) collective-permute-start(bf16[96,1024]{1,0:T(8,128)(2,1)S(1)} %copy-done.2), channel_id=1, source_target_pairs={{0,2},{2,0},{4,6},{6,4},{8,10},{10,8},{12,14},{14,12},{16,18},{18,... | collective-permute-start | bytes 589832 | tf_op jit(solution)/shard_map/ppermute | solution.py:213
  26.1 0.0 collective-permute-done.9.refs_15_
  26.1 0.1 collective-permute-start.14
  26.2 4.1 %collective-permute-start.8 = (bf16[96,1024]{1,0:T(8,128)(2,1)S(1)}, bf16[96,1024]{1,0:T(8,128)(2,1)S(1)}, u32[]{:S(2)}, u32[]{:S(2)}) collective-permute-start(bf16[96,1024]{1,0:T(8,128)(2,1)S(1)} %collective-permute-done.5.refs_11_), channel_id=1, source_target_pairs={{0,4},{2,6},{4,0},{6,2},{8,12},{10,14},{12,8},{14,10},{16,20},{18,... | collective-permute-start | bytes 589832 | tf_op jit(solution)/shard_map/ppermute | solution.py:213
  30.3 0.7 collective-permute-start.4
  31.0 0.0 collective-permute-done.7.refs_13_
  31.0 0.0 collective-permute-start.3
  31.0 0.0 collective-permute-done.2.refs_8_
  31.0 0.5 collective-permute-start.10
  31.5 0.0 collective-permute-done.14.refs_20_
  31.5 0.1 collective-permute-start.11
  31.6 3.6 %collective-permute-done.8.refs_14_ = bf16[96,1024]{1,0:T(8,128)(2,1)S(1)} collective-permute-done((bf16[96,1024]{1,0:T(8,128)(2,1)S(1)}, bf16[96,1024]{1,0:T(8,128)(2,1)S(1)}, u32[]{:S(2)}, u32[]{:S(2)}) %collective-permute-start.8) | collective-permute-done | bytes 196640 | tf_op jit(solution)/shard_map/ppermute | solution.py:213
  35.2 0.9 %collective-permute-start.13 = (bf16[96,1024]{1,0:T(8,128)(2,1)S(1)}, bf16[96,1024]{1,0:T(8,128)(2,1)S(1)}, u32[]{:S(2)}, u32[]{:S(2)}) collective-permute-start(bf16[96,1024]{1,0:T(8,128)(2,1)S(1)} %collective-permute-done.8.refs_14_), channel_id=1, source_target_pairs={{0,2},{2,0},{4,6},{6,4},{8,10},{10,8},{12,14},{14,12},{16,18},{18,... | collective-permute-start | bytes 589832 | tf_op jit(solution)/shard_map/ppermute | solution.py:213
  36.2 0.0 collective-permute-done.4.refs_10_
  36.2 0.0 collective-permute-start.12
  36.2 0.0 collective-permute-done.3.refs_9_
  36.2 4.0 %collective-permute-start.17 = (bf16[512,1024]{1,0:T(8,128)(2,1)}, bf16[512,1024]{1,0:T(8,128)(2,1)S(1)}, u32[]{:S(2)}, u32[]{:S(2)}) collective-permute-start(bf16[512,1024]{1,0:T(8,128)(2,1)} %copy-done.3), channel_id=1, source_target_pairs={{0,2},{2,4},{4,6},{6,8},{8,10},{10,12},{12,14},{14,16},{16,18},{18... | collective-permute-start | bytes 3145736 | tf_op jit(solution)/shard_map/ppermute | solution.py:233
  40.2 0.0 collective-permute-done.11.refs_17_
  40.2 0.0 collective-permute-done.10.refs_16_
  40.2 0.0 collective-permute-done.13.refs_19_
  40.2 0.0 collective-permute-done.12.refs_18_
  40.2 4.0 %shard_map.48 = bf16[128,1024]{1,0:T(8,128)(2,1)S(1)} custom-call(bf16[768,1024]{1,0:T(8,128)(2,1)} %refs_0_.8, bf16[768,1024]{1,0:T(8,128)(2,1)} %refs_3_.9, bf16[768,1024]{1,0:T(8,128)(2,1)} %refs_4_.9, bf16[768,1024]{1,0:T(8,128)(2,1)} %refs_3_.9, bf16[768,1024]{1,0:T(8,128)(2,1)} %refs_4_.9, bf16[96,1024]{1,0:T(8,128)(2,1)S(1)} %copy-done.2, ...), custom_call_target="tpu_custom_call" | custom-call | flops 671088640 | bytes 5242880 | tf_op jit(solution)/shard_map/pallas_call | solution.py:151
  44.2 0.5 fusion.28
  44.7 1.3 %collective-permute-start.15 = (bf16[128,1024]{1,0:T(8,128)(2,1)S(1)}, bf16[128,1024]{1,0:T(8,128)(2,1)S(1)}, u32[]{:S(2)}, u32[]{:S(2)}) collective-permute-start(bf16[128,1024]{1,0:T(8,128)(2,1)S(1)} %fusion.28), channel_id=1, source_target_pairs={{0,1},{1,0},{2,3},{3,2},{4,5},{5,4},{6,7},{7,6},{8,9},{9,8},{10,11... | collective-permute-start | bytes 786440 | tf_op jit(solution)/shard_map/ppermute | solution.py:258
  45.9 3.9 %shard_map.49 = bf16[128,1024]{1,0:T(8,128)(2,1)S(1)} custom-call(bf16[768,1024]{1,0:T(8,128)(2,1)} %refs_0_.8, bf16[768,1024]{1,0:T(8,128)(2,1)} %refs_3_.9, bf16[768,1024]{1,0:T(8,128)(2,1)} %refs_4_.9, bf16[768,1024]{1,0:T(8,128)(2,1)} %refs_3_.9, bf16[768,1024]{1,0:T(8,128)(2,1)} %refs_4_.9, bf16[96,1024]{1,0:T(8,128)(2,1)S(1)} %copy-done.2, ...), custom_call_target="tpu_custom_call" | custom-call | flops 671088640 | bytes 5242880 | tf_op jit(solution)/shard_map/pallas_call | solution.py:151
  49.9 0.5 fusion.31
  50.3 0.3 collective-permute-start.16
  50.7 0.4 fusion.34.refs_1_
  51.1 1.1 %collective-permute-done.15.refs_0_ = bf16[128,1024]{1,0:T(8,128)(2,1)S(1)} collective-permute-done((bf16[128,1024]{1,0:T(8,128)(2,1)S(1)}, bf16[128,1024]{1,0:T(8,128)(2,1)S(1)}, u32[]{:S(2)}, u32[]{:S(2)}) %collective-permute-start.15) | collective-permute-done | bytes 262176 | tf_op jit(solution)/shard_map/ppermute | solution.py:258
  52.2 5.8 %shard_map.50 = bf16[256,1024]{1,0:T(8,128)(2,1)S(1)} custom-call(bf16[768,1024]{1,0:T(8,128)(2,1)} %refs_0_.8, bf16[768,1024]{1,0:T(8,128)(2,1)} %refs_3_.9, bf16[768,1024]{1,0:T(8,128)(2,1)} %refs_4_.9, bf16[768,1024]{1,0:T(8,128)(2,1)} %refs_3_.9, bf16[768,1024]{1,0:T(8,128)(2,1)} %refs_4_.9, bf16[96,1024]{1,0:T(8,128)(2,1)S(1)} %copy-done.2, ...), custom_call_target="tpu_custom_call" | custom-call | flops 1342177280 | bytes 5242880 | tf_op jit(solution)/shard_map/pallas_call | solution.py:151
  58.0 0.7 fusion.16
  58.7 1.8 %collective-permute-start.19 = (bf16[256,1024]{1,0:T(8,128)(2,1)S(1)}, bf16[256,1024]{1,0:T(8,128)(2,1)S(1)}, u32[]{:S(2)}, u32[]{:S(2)}) collective-permute-start(bf16[256,1024]{1,0:T(8,128)(2,1)S(1)} %fusion.16), channel_id=1, source_target_pairs={{0,1},{1,0},{2,3},{3,2},{4,5},{5,4},{6,7},{7,6},{8,9},{9,8},{10,11... | collective-permute-start | bytes 1572872 | tf_op jit(solution)/shard_map/ppermute | solution.py:258
  60.5 0.0 collective-permute-done.16.refs_0_
  60.5 0.0 collective-permute-done.17.refs_1_.refs_2_
  60.5 1.0 %copy-done.5 = bf16[512,1024]{1,0:T(8,128)(2,1)} copy-done((bf16[512,1024]{1,0:T(8,128)(2,1)}, bf16[512,1024]{1,0:T(8,128)(2,1)S(1)}, u32[]{:S(2)}) %copy-start.5) | copy-done | bytes 1048600
  61.5 5.8 %shard_map.51 = bf16[256,1024]{1,0:T(8,128)(2,1)S(1)} custom-call(bf16[768,1024]{1,0:T(8,128)(2,1)} %refs_0_.8, bf16[512,1024]{1,0:T(8,128)(2,1)} %copy-done.5, bf16[512,1024]{1,0:T(8,128)(2,1)} %copy-done.5, bf16[768,1024]{1,0:T(8,128)(2,1)} %refs_3_.9, bf16[768,1024]{1,0:T(8,128)(2,1)} %refs_4_.9, bf16[96,1024]{1,0:T(8,128)(2,1)S(1)} %copy-done.2, ...), custom_call_target="tpu_custom_call" | custom-call | flops 1342177280 | bytes 5242880 | tf_op jit(solution)/shard_map/pallas_call | solution.py:151
  67.3 0.7 fusion.19
  68.0 0.1 collective-permute-start.18
  68.1 0.4 fusion.37.refs_1_
  68.6 0.7 fusion.22.refs_1_
  69.3 0.7 fusion.25.refs_1_
  70.0 0.8 shard_map.52.refs_2_
  70.8 0.8 shard_map.53.refs_2_
  71.5 1.5 %collective-permute-done.19.refs_0_ = bf16[256,1024]{1,0:T(8,128)(2,1)S(1)} collective-permute-done((bf16[256,1024]{1,0:T(8,128)(2,1)S(1)}, bf16[256,1024]{1,0:T(8,128)(2,1)S(1)}, u32[]{:S(2)}, u32[]{:S(2)}) %collective-permute-start.19) | collective-permute-done | bytes 524320 | tf_op jit(solution)/shard_map/ppermute | solution.py:258
  73.0 0.9 %shard_map.54.refs_2_ = bf16[768,1024]{1,0:T(8,128)(2,1)} custom-call(bf16[256,1024]{1,0:T(8,128)(2,1)S(1)} %collective-permute-done.19.refs_0_, bf16[256,1024]{1,0:T(8,128)(2,1)S(1)} %fusion.22.refs_1_, bf16[768,1024]{1,0:T(8,128)(2,1)} %shard_map.53.refs_2_), custom_call_target="tpu_custom_call", output_to_operand_aliasing={{}: (2, {})} | custom-call | bytes 2097152 | tf_op jit(solution)/shard_map/pallas_call | solution.py:177
  73.9 9.7 %collective-permute-done.18.refs_0_ = bf16[256,1024]{1,0:T(8,128)(2,1)S(1)} collective-permute-done((bf16[256,1024]{1,0:T(8,128)(2,1)S(1)}, bf16[256,1024]{1,0:T(8,128)(2,1)S(1)}, u32[]{:S(2)}, u32[]{:S(2)}) %collective-permute-start.18) | collective-permute-done | bytes 524320 | tf_op jit(solution)/shard_map/ppermute | solution.py:258
  83.6 0.9 %shard_map.55 = bf16[768,1024]{1,0:T(8,128)(2,1)} custom-call(bf16[256,1024]{1,0:T(8,128)(2,1)S(1)} %collective-permute-done.18.refs_0_, bf16[256,1024]{1,0:T(8,128)(2,1)S(1)} %fusion.25.refs_1_, bf16[768,1024]{1,0:T(8,128)(2,1)} %shard_map.54.refs_2_), custom_call_target="tpu_custom_call", output_to_operand_aliasing={{}: (2, {})} | custom-call | bytes 2097152 | tf_op jit(solution)/shard_map/pallas_call | solution.py:177
  (6 shorter events, 0.0 us)
Async XLA Ops:
  0.0 14.5 %copy-start = (bf16[768,1024]{1,0:T(8,128)(2,1)S(1)}, bf16[768,1024]{1,0:T(8,128)(2,1)}, u32[]{:S(2)}) copy-start(bf16[768,1024]{1,0:T(8,128)(2,1)} %refs_3_.9) | copy-start | bytes 4718596
  1.6 6.0 %collective-permute-start.1 = (bf16[96,1024]{1,0:T(8,128)(2,1)}, bf16[96,1024]{1,0:T(8,128)(2,1)S(1)}, u32[]{:S(2)}, u32[]{:S(2)}) collective-permute-start(bf16[96,1024]{1,0:T(8,128)(2,1)} %shard_map.46.refs_5_), channel_id=1, source_target_pairs={{0,4},{2,6},{4,0},{6,2},{8,12},{10,14},{12,8},{14,10},{16,20},{18,... | collective-permute-start | bytes 589832 | tf_op jit(solution)/shard_map/ppermute | solution.py:213
  2.9 7.5 %collective-permute-start = (bf16[96,1024]{1,0:T(8,128)(2,1)}, bf16[96,1024]{1,0:T(8,128)(2,1)S(1)}, u32[]{:S(2)}, u32[]{:S(2)}) collective-permute-start(bf16[96,1024]{1,0:T(8,128)(2,1)} %shard_map.46.refs_5_), channel_id=1, source_target_pairs={{0,8},{2,10},{4,12},{6,14},{8,16},{10,18},{12,20},{14,22},{16,24},... | collective-permute-start | bytes 589832 | tf_op jit(solution)/shard_map/ppermute | solution.py:213
  10.4 6.6 %collective-permute-start.6 = (bf16[96,1024]{1,0:T(8,128)(2,1)S(1)}, bf16[96,1024]{1,0:T(8,128)(2,1)S(1)}, u32[]{:S(2)}, u32[]{:S(2)}) collective-permute-start(bf16[96,1024]{1,0:T(8,128)(2,1)S(1)} %collective-permute-done.refs_6_), channel_id=1, source_target_pairs={{0,4},{2,6},{4,0},{6,2},{8,12},{10,14},{12,8},{14,10},{16,20},{18,... | collective-permute-start | bytes 589832 | tf_op jit(solution)/shard_map/ppermute | solution.py:213
  10.7 6.7 %collective-permute-start.5 = (bf16[96,1024]{1,0:T(8,128)(2,1)S(1)}, bf16[96,1024]{1,0:T(8,128)(2,1)S(1)}, u32[]{:S(2)}, u32[]{:S(2)}) collective-permute-start(bf16[96,1024]{1,0:T(8,128)(2,1)S(1)} %collective-permute-done.refs_6_), channel_id=1, source_target_pairs={{8,16},{10,18},{12,20},{14,22},{16,24},{18,26},{20,28},{22,30},{9,... | collective-permute-start | bytes 589832 | tf_op jit(solution)/shard_map/ppermute | solution.py:213
  13.9 12.2 %collective-permute-start.9 = (bf16[96,1024]{1,0:T(8,128)(2,1)}, bf16[96,1024]{1,0:T(8,128)(2,1)S(1)}, u32[]{:S(2)}, u32[]{:S(2)}) collective-permute-start(bf16[96,1024]{1,0:T(8,128)(2,1)} %shard_map.46.refs_5_), channel_id=1, source_target_pairs={{0,28},{2,30},{4,24},{6,26},{1,29},{3,31},{5,25},{7,27}} | collective-permute-start | bytes 589832 | tf_op jit(solution)/shard_map/ppermute | solution.py:213
  14.6 1.4 %copy-start.1 = (bf16[768,1024]{1,0:T(8,128)(2,1)S(1)}, bf16[768,1024]{1,0:T(8,128)(2,1)}, u32[]{:S(2)}) copy-start(bf16[768,1024]{1,0:T(8,128)(2,1)} %refs_4_.9) | copy-start | bytes 4718596
  16.0 4.6 %copy-start.2 = (bf16[96,1024]{1,0:T(8,128)(2,1)S(1)}, bf16[96,1024]{1,0:T(8,128)(2,1)}, u32[]{:S(2)}) copy-start(bf16[96,1024]{1,0:T(8,128)(2,1)} %shard_map.46.refs_5_) | copy-start | bytes 589828
  16.0 1.0 %copy-start.3 = (bf16[512,1024]{1,0:T(8,128)(2,1)}, bf16[512,1024]{1,0:T(8,128)(2,1)S(1)}, u32[]{:S(2)}) copy-start(bf16[512,1024]{1,0:T(8,128)(2,1)S(1)} %shard_map.47) | copy-start | bytes 3145732
  17.4 13.7 %collective-permute-start.7 = (bf16[96,1024]{1,0:T(8,128)(2,1)S(1)}, bf16[96,1024]{1,0:T(8,128)(2,1)S(1)}, u32[]{:S(2)}, u32[]{:S(2)}) collective-permute-start(bf16[96,1024]{1,0:T(8,128)(2,1)S(1)} %collective-permute-done.5.refs_11_), channel_id=1, source_target_pairs={{16,24},{18,26},{20,28},{22,30},{17,25},{19,27},{21,29},{23,31}} | collective-permute-start | bytes 589832 | tf_op jit(solution)/shard_map/ppermute | solution.py:213
  20.6 10.4 %collective-permute-start.2 = (bf16[96,1024]{1,0:T(8,128)(2,1)S(1)}, bf16[96,1024]{1,0:T(8,128)(2,1)S(1)}, u32[]{:S(2)}, u32[]{:S(2)}) collective-permute-start(bf16[96,1024]{1,0:T(8,128)(2,1)S(1)} %copy-done.2), channel_id=1, source_target_pairs={{0,2},{2,0},{4,6},{6,4},{8,10},{10,8},{12,14},{14,12},{16,18},{18,... | collective-permute-start | bytes 589832 | tf_op jit(solution)/shard_map/ppermute | solution.py:213
  26.1 5.4 %collective-permute-start.14 = (bf16[96,1024]{1,0:T(8,128)(2,1)S(1)}, bf16[96,1024]{1,0:T(8,128)(2,1)S(1)}, u32[]{:S(2)}, u32[]{:S(2)}) collective-permute-start(bf16[96,1024]{1,0:T(8,128)(2,1)S(1)} %collective-permute-done.9.refs_15_), channel_id=1, source_target_pairs={{0,2},{2,0},{4,6},{6,4},{8,10},{10,8},{12,14},{14,12},{16,18},{18,... | collective-permute-start | bytes 589832 | tf_op jit(solution)/shard_map/ppermute | solution.py:213
  26.2 9.0 %collective-permute-start.8 = (bf16[96,1024]{1,0:T(8,128)(2,1)S(1)}, bf16[96,1024]{1,0:T(8,128)(2,1)S(1)}, u32[]{:S(2)}, u32[]{:S(2)}) collective-permute-start(bf16[96,1024]{1,0:T(8,128)(2,1)S(1)} %collective-permute-done.5.refs_11_), channel_id=1, source_target_pairs={{0,4},{2,6},{4,0},{6,2},{8,12},{10,14},{12,8},{14,10},{16,20},{18,... | collective-permute-start | bytes 589832 | tf_op jit(solution)/shard_map/ppermute | solution.py:213
  30.3 5.9 %collective-permute-start.4 = (bf16[96,1024]{1,0:T(8,128)(2,1)S(1)}, bf16[96,1024]{1,0:T(8,128)(2,1)S(1)}, u32[]{:S(2)}, u32[]{:S(2)}) collective-permute-start(bf16[96,1024]{1,0:T(8,128)(2,1)S(1)} %collective-permute-done.1.refs_7_), channel_id=1, source_target_pairs={{0,2},{2,0},{4,6},{6,4},{8,10},{10,8},{12,14},{14,12},{16,18},{18,... | collective-permute-start | bytes 589832 | tf_op jit(solution)/shard_map/ppermute | solution.py:213
  31.0 5.2 %collective-permute-start.3 = (bf16[96,1024]{1,0:T(8,128)(2,1)S(1)}, bf16[96,1024]{1,0:T(8,128)(2,1)S(1)}, u32[]{:S(2)}, u32[]{:S(2)}) collective-permute-start(bf16[96,1024]{1,0:T(8,128)(2,1)S(1)} %collective-permute-done.refs_6_), channel_id=1, source_target_pairs={{0,2},{2,0},{4,6},{6,4},{8,10},{10,8},{12,14},{14,12},{16,18},{18,... | collective-permute-start | bytes 589832 | tf_op jit(solution)/shard_map/ppermute | solution.py:213
  31.0 9.2 %collective-permute-start.10 = (bf16[96,1024]{1,0:T(8,128)(2,1)S(1)}, bf16[96,1024]{1,0:T(8,128)(2,1)S(1)}, u32[]{:S(2)}, u32[]{:S(2)}) collective-permute-start(bf16[96,1024]{1,0:T(8,128)(2,1)S(1)} %collective-permute-done.5.refs_11_), channel_id=1, source_target_pairs={{0,2},{2,0},{4,6},{6,4},{8,10},{10,8},{12,14},{14,12},{16,18},{18,... | collective-permute-start | bytes 589832 | tf_op jit(solution)/shard_map/ppermute | solution.py:213
  31.5 8.7 %collective-permute-start.11 = (bf16[96,1024]{1,0:T(8,128)(2,1)S(1)}, bf16[96,1024]{1,0:T(8,128)(2,1)S(1)}, u32[]{:S(2)}, u32[]{:S(2)}) collective-permute-start(bf16[96,1024]{1,0:T(8,128)(2,1)S(1)} %collective-permute-done.6.refs_12_), channel_id=1, source_target_pairs={{0,2},{2,0},{4,6},{6,4},{8,10},{10,8},{12,14},{14,12},{16,18},{18,... | collective-permute-start | bytes 589832 | tf_op jit(solution)/shard_map/ppermute | solution.py:213
  35.2 5.0 %collective-permute-start.13 = (bf16[96,1024]{1,0:T(8,128)(2,1)S(1)}, bf16[96,1024]{1,0:T(8,128)(2,1)S(1)}, u32[]{:S(2)}, u32[]{:S(2)}) collective-permute-start(bf16[96,1024]{1,0:T(8,128)(2,1)S(1)} %collective-permute-done.8.refs_14_), channel_id=1, source_target_pairs={{0,2},{2,0},{4,6},{6,4},{8,10},{10,8},{12,14},{14,12},{16,18},{18,... | collective-permute-start | bytes 589832 | tf_op jit(solution)/shard_map/ppermute | solution.py:213
  36.2 4.1 %collective-permute-start.12 = (bf16[96,1024]{1,0:T(8,128)(2,1)S(1)}, bf16[96,1024]{1,0:T(8,128)(2,1)S(1)}, u32[]{:S(2)}, u32[]{:S(2)}) collective-permute-start(bf16[96,1024]{1,0:T(8,128)(2,1)S(1)} %collective-permute-done.7.refs_13_), channel_id=1, source_target_pairs={{0,2},{2,0},{4,6},{6,4},{8,10},{10,8},{12,14},{14,12},{16,18},{18,... | collective-permute-start | bytes 589832 | tf_op jit(solution)/shard_map/ppermute | solution.py:213
  36.2 8.0 %copy-start.4 = (bf16[1024,2048]{1,0:T(8,128)(2,1)S(1)}, bf16[1024,2048]{1,0:T(8,128)(2,1)}, u32[]{:S(2)}) copy-start(bf16[1024,2048]{1,0:T(8,128)(2,1)} %param.7) | copy-start | bytes 12582916
  36.2 24.3 %collective-permute-start.17 = (bf16[512,1024]{1,0:T(8,128)(2,1)}, bf16[512,1024]{1,0:T(8,128)(2,1)S(1)}, u32[]{:S(2)}, u32[]{:S(2)}) collective-permute-start(bf16[512,1024]{1,0:T(8,128)(2,1)} %copy-done.3), channel_id=1, source_target_pairs={{0,2},{2,4},{4,6},{6,8},{8,10},{10,12},{12,14},{14,16},{16,18},{18... | collective-permute-start | bytes 3145736 | tf_op jit(solution)/shard_map/ppermute | solution.py:233
  44.7 7.5 %collective-permute-start.15 = (bf16[128,1024]{1,0:T(8,128)(2,1)S(1)}, bf16[128,1024]{1,0:T(8,128)(2,1)S(1)}, u32[]{:S(2)}, u32[]{:S(2)}) collective-permute-start(bf16[128,1024]{1,0:T(8,128)(2,1)S(1)} %fusion.28), channel_id=1, source_target_pairs={{0,1},{1,0},{2,3},{3,2},{4,5},{5,4},{6,7},{7,6},{8,9},{9,8},{10,11... | collective-permute-start | bytes 786440 | tf_op jit(solution)/shard_map/ppermute | solution.py:258
  50.3 10.2 %collective-permute-start.16 = (bf16[128,1024]{1,0:T(8,128)(2,1)S(1)}, bf16[128,1024]{1,0:T(8,128)(2,1)S(1)}, u32[]{:S(2)}, u32[]{:S(2)}) collective-permute-start(bf16[128,1024]{1,0:T(8,128)(2,1)S(1)} %fusion.31), channel_id=1, source_target_pairs={{0,1},{1,0},{2,3},{3,2},{4,5},{5,4},{6,7},{7,6},{8,9},{9,8},{10,11... | collective-permute-start | bytes 786440 | tf_op jit(solution)/shard_map/ppermute | solution.py:258
  58.7 14.3 %collective-permute-start.19 = (bf16[256,1024]{1,0:T(8,128)(2,1)S(1)}, bf16[256,1024]{1,0:T(8,128)(2,1)S(1)}, u32[]{:S(2)}, u32[]{:S(2)}) collective-permute-start(bf16[256,1024]{1,0:T(8,128)(2,1)S(1)} %fusion.16), channel_id=1, source_target_pairs={{0,1},{1,0},{2,3},{3,2},{4,5},{5,4},{6,7},{7,6},{8,9},{9,8},{10,11... | collective-permute-start | bytes 1572872 | tf_op jit(solution)/shard_map/ppermute | solution.py:258
  60.5 1.0 %copy-start.5 = (bf16[512,1024]{1,0:T(8,128)(2,1)}, bf16[512,1024]{1,0:T(8,128)(2,1)S(1)}, u32[]{:S(2)}) copy-start(bf16[512,1024]{1,0:T(8,128)(2,1)S(1)} %collective-permute-done.17.refs_1_.refs_2_) | copy-start | bytes 3145732
  68.0 15.6 %collective-permute-start.18 = (bf16[256,1024]{1,0:T(8,128)(2,1)S(1)}, bf16[256,1024]{1,0:T(8,128)(2,1)S(1)}, u32[]{:S(2)}, u32[]{:S(2)}) collective-permute-start(bf16[256,1024]{1,0:T(8,128)(2,1)S(1)} %fusion.19), channel_id=1, source_target_pairs={{0,1},{1,0},{2,3},{3,2},{4,5},{5,4},{6,7},{7,6},{8,9},{9,8},{10,11... | collective-permute-start | bytes 1572872 | tf_op jit(solution)/shard_map/ppermute | solution.py:258

commit v3 on v2

--- a/solution.py
+++ b/solution.py
@@ -224,10 +224,10 @@
         z2, y1 = up(z1, 2), flip(z1, 2)
         z2, y1, tail = tie((z2, y1, tail_rows(keys, values)))
         z3, y2 = up(z2, 3), flip(z2, 2)
-        z3, tail = tie((z3, tail))
+        z3, tail, own, z1, y0, z2, y1 = tie((z3, tail, own, z1, y0, z2, y1))
         early = {(0, 0, 0): own, (1, 0, 0): z1, (0, 1, 0): y0}
+        late = {(2, 0, 0): z2, (1, 1, 0): y1, (3, 0, 0): z3, (2, 1, 0): y2, (3, 1, 0): far}
         early |= {(k, y, 1): flip(p, 1) for (k, y, _), p in list(early.items())}
-        late = {(2, 0, 0): z2, (1, 1, 0): y1, (3, 0, 0): z3, (2, 1, 0): y2, (3, 1, 0): far}
         late |= {(k, y, 1): flip(p, 1) for (k, y, _), p in list(late.items())}
 
     rim = lax.ppermute(tail, "ctx", [(i, i + 1) for i in range(n_ctx - 1)])

time: 84.9 us -> 82.7 us (0.974)
  the two profiles are of different devices: /device:TPU:17 before, /device:TPU:26 now
where the time goes in v3:
time: 82.7 us; the launch traced here: 82.3 us
  waiting for transfers between devices  30 us (36%)
  Pallas kernels  24.5 us (30%)
  starting transfers between devices  19.6 us (24%)
  matrix products  4.67 us (6%)
  local copies, waits for them, and re-layouts  3.34 us (4%)
    pallas_call x4, Pallas kernels, attend(): pl.pallas_call(functools.partial(attend_kernel, cfg), grid=(steps,), in_s...  19.4 us
    ppermute x15, waiting for transfers between devices, send(): return lax.ppermute(value, 'ctx', pairs)  18.4 us
    ppermute x15, starting transfers between devices, send(): return lax.ppermute(value, 'ctx', pairs)  12.9 us
    ppermute x4, waiting for transfers between devices, per_device(): lax.ppermute(value, 'head', [(i, (i + step) % n_head) for i in range(n_he...  11.6 us
    dot_general x8, matrix products, partial(): jnp.dot(att, w, preferred_element_type=jnp.float32).astype(jnp.bfloat16)  4.67 us
    ppermute x4, starting transfers between devices, per_device(): lax.ppermute(value, 'head', [(i, (i + step) % n_head) for i in range(n_he...  4.29 us
    pallas_call x4, Pallas kernels, add_into(): pl.pallas_call(functools.partial(add_kernel, len(parts)), grid=(1,), in_s...  3.36 us
    unnamed x12, local copies, waits for them, and re-layouts  3.34 us
  transfers between devices with their start and end apart: 20, of which 11 were waited for; matrix products, arithmetic and copies ran while one was open for 6% of the time, Pallas kernels for 27%

profile of v3, /device:TPU:26, one launch (start us, length us, event | category | flops | bytes accessed | tf_op | source)
XLA Modules:
  0.0 82.3 jit_solution(17444663337588683015)
XLA Ops:
  0.0 1.6 %shard_map.46.refs_5_ = bf16[96,1024]{1,0:T(8,128)(2,1)} custom-call(bf16[768,1024]{1,0:T(8,128)(2,1)} %refs_3_.9, bf16[768,1024]{1,0:T(8,128)(2,1)} %refs_3_.9, bf16[768,1024]{1,0:T(8,128)(2,1)} %refs_3_.9, bf16[768,1024]{1,0:T(8,128)(2,1)} %refs_4_.9, bf16[768,1024]{1,0:T(8,128)(2,1)} %refs_4_.9, bf16[768,1024]{1,0:T(8,128)(2,1)} %refs_4_.9), custom_call_target="tpu_custom_call" | custom-call | bytes 393216 | tf_op jit(solution)/shard_map/pallas_call | solution.py:30
  1.6 1.5 %collective-permute-start.1 = (bf16[96,1024]{1,0:T(8,128)(2,1)}, bf16[96,1024]{1,0:T(8,128)(2,1)S(1)}, u32[]{:S(2)}, u32[]{:S(2)}) collective-permute-start(bf16[96,1024]{1,0:T(8,128)(2,1)} %shard_map.46.refs_5_), channel_id=1, source_target_pairs={{0,4},{2,6},{4,0},{6,2},{8,12},{10,14},{12,8},{14,10},{16,20},{18,... | collective-permute-start | bytes 589832 | tf_op jit(solution)/shard_map/ppermute | solution.py:213
  3.2 1.3 %collective-permute-start = (bf16[96,1024]{1,0:T(8,128)(2,1)}, bf16[96,1024]{1,0:T(8,128)(2,1)S(1)}, u32[]{:S(2)}, u32[]{:S(2)}) collective-permute-start(bf16[96,1024]{1,0:T(8,128)(2,1)} %shard_map.46.refs_5_), channel_id=1, source_target_pairs={{0,8},{2,10},{4,12},{6,14},{8,16},{10,18},{12,20},{14,22},{16,24},... | collective-permute-start | bytes 589832 | tf_op jit(solution)/shard_map/ppermute | solution.py:213
  4.5 4.0 %collective-permute-done.1.refs_7_ = bf16[96,1024]{1,0:T(8,128)(2,1)S(1)} collective-permute-done((bf16[96,1024]{1,0:T(8,128)(2,1)}, bf16[96,1024]{1,0:T(8,128)(2,1)S(1)}, u32[]{:S(2)}, u32[]{:S(2)}) %collective-permute-start.1) | collective-permute-done | bytes 196640 | tf_op jit(solution)/shard_map/ppermute | solution.py:213
  8.5 3.1 %collective-permute-done.refs_6_ = bf16[96,1024]{1,0:T(8,128)(2,1)S(1)} collective-permute-done((bf16[96,1024]{1,0:T(8,128)(2,1)}, bf16[96,1024]{1,0:T(8,128)(2,1)S(1)}, u32[]{:S(2)}, u32[]{:S(2)}) %collective-permute-start) | collective-permute-done | bytes 196640 | tf_op jit(solution)/shard_map/ppermute | solution.py:213
  11.6 0.5 collective-permute-start.3
  12.1 1.3 %collective-permute-start.2 = (bf16[96,1024]{1,0:T(8,128)(2,1)S(1)}, bf16[96,1024]{1,0:T(8,128)(2,1)S(1)}, u32[]{:S(2)}, u32[]{:S(2)}) collective-permute-start(bf16[96,1024]{1,0:T(8,128)(2,1)S(1)} %collective-permute-done.refs_6_), channel_id=1, source_target_pairs={{8,16},{10,18},{12,20},{14,22},{16,24},{18,26},{20,28},{22,30},{9,... | collective-permute-start | bytes 589832 | tf_op jit(solution)/shard_map/ppermute | solution.py:213
  13.4 1.3 %collective-permute-start.9 = (bf16[96,1024]{1,0:T(8,128)(2,1)}, bf16[96,1024]{1,0:T(8,128)(2,1)S(1)}, u32[]{:S(2)}, u32[]{:S(2)}) collective-permute-start(bf16[96,1024]{1,0:T(8,128)(2,1)} %shard_map.46.refs_5_), channel_id=1, source_target_pairs={{0,28},{2,30},{4,24},{6,26},{1,29},{3,31},{5,25},{7,27}} | collective-permute-start | bytes 589832 | tf_op jit(solution)/shard_map/ppermute | solution.py:213
  14.7 0.0 copy-start.1
  14.7 1.4 %copy-done.1 = bf16[768,1024]{1,0:T(8,128)(2,1)S(1)} copy-done((bf16[768,1024]{1,0:T(8,128)(2,1)S(1)}, bf16[768,1024]{1,0:T(8,128)(2,1)}, u32[]{:S(2)}) %copy-start.1) | copy-done | bytes 1572888
  16.1 0.1 shard_map.47
  16.2 0.0 copy-start.3
  16.2 1.0 %copy-done.3 = bf16[512,1024]{1,0:T(8,128)(2,1)} copy-done((bf16[512,1024]{1,0:T(8,128)(2,1)}, bf16[512,1024]{1,0:T(8,128)(2,1)S(1)}, u32[]{:S(2)}) %copy-start.3) | copy-done | bytes 1048600
  17.2 0.1 collective-permute-done.3.refs_12_
  17.3 4.5 %collective-permute-done.2.refs_11_ = bf16[96,1024]{1,0:T(8,128)(2,1)S(1)} collective-permute-done((bf16[96,1024]{1,0:T(8,128)(2,1)S(1)}, bf16[96,1024]{1,0:T(8,128)(2,1)S(1)}, u32[]{:S(2)}, u32[]{:S(2)}) %collective-permute-start.2) | collective-permute-done | bytes 196640 | tf_op jit(solution)/shard_map/ppermute | solution.py:213
  21.8 4.4 %collective-permute-start.8 = (bf16[96,1024]{1,0:T(8,128)(2,1)S(1)}, bf16[96,1024]{1,0:T(8,128)(2,1)S(1)}, u32[]{:S(2)}, u32[]{:S(2)}) collective-permute-start(bf16[96,1024]{1,0:T(8,128)(2,1)S(1)} %collective-permute-done.2.refs_11_), channel_id=1, source_target_pairs={{0,4},{2,6},{4,0},{6,2},{8,12},{10,14},{12,8},{14,10},{16,20},{18,... | collective-permute-start | bytes 589832 | tf_op jit(solution)/shard_map/ppermute | solution.py:213
  26.2 1.3 %collective-permute-start.4 = (bf16[96,1024]{1,0:T(8,128)(2,1)S(1)}, bf16[96,1024]{1,0:T(8,128)(2,1)S(1)}, u32[]{:S(2)}, u32[]{:S(2)}) collective-permute-start(bf16[96,1024]{1,0:T(8,128)(2,1)S(1)} %collective-permute-done.2.refs_11_), channel_id=1, source_target_pairs={{16,24},{18,26},{20,28},{22,30},{17,25},{19,27},{21,29},{23,31}} | collective-permute-start | bytes 589832 | tf_op jit(solution)/shard_map/ppermute | solution.py:213
  27.5 0.0 collective-permute-done.9.refs_15_
  27.5 0.1 collective-permute-start.14
  27.6 2.3 %collective-permute-done.8.refs_14_ = bf16[96,1024]{1,0:T(8,128)(2,1)S(1)} collective-permute-done((bf16[96,1024]{1,0:T(8,128)(2,1)S(1)}, bf16[96,1024]{1,0:T(8,128)(2,1)S(1)}, u32[]{:S(2)}, u32[]{:S(2)}) %collective-permute-start.8) | collective-permute-done | bytes 196640 | tf_op jit(solution)/shard_map/ppermute | solution.py:213
  29.9 0.0 collective-permute-start.13
  29.9 3.9 %collective-permute-done.4.refs_13_ = bf16[96,1024]{1,0:T(8,128)(2,1)S(1)} collective-permute-done((bf16[96,1024]{1,0:T(8,128)(2,1)S(1)}, bf16[96,1024]{1,0:T(8,128)(2,1)S(1)}, u32[]{:S(2)}, u32[]{:S(2)}) %collective-permute-start.4) | collective-permute-done | bytes 196640 | tf_op jit(solution)/shard_map/ppermute | solution.py:213
  33.8 0.0 collective-permute-start.5
  33.8 0.5 collective-permute-start.6
  34.3 0.0 collective-permute-start.7
  34.3 0.0 collective-permute-done.14.refs_20_
  34.3 0.5 collective-permute-start.10
  34.8 0.0 collective-permute-done.13.refs_19_
  34.8 0.1 collective-permute-start.11
  34.9 0.3 collective-permute-done.5.refs_8_
  35.2 0.1 collective-permute-start.12
  35.3 0.1 collective-permute-done.6.refs_9_
  35.5 2.4 %collective-permute-start.17 = (bf16[512,1024]{1,0:T(8,128)(2,1)}, bf16[512,1024]{1,0:T(8,128)(2,1)S(1)}, u32[]{:S(2)}, u32[]{:S(2)}) collective-permute-start(bf16[512,1024]{1,0:T(8,128)(2,1)} %copy-done.3), channel_id=1, source_target_pairs={{0,2},{2,4},{4,6},{6,8},{8,10},{10,12},{12,14},{14,16},{16,18},{18... | collective-permute-start | bytes 3145736 | tf_op jit(solution)/shard_map/ppermute | solution.py:233
  37.9 0.0 collective-permute-done.7.refs_10_
  37.9 0.0 collective-permute-done.10.refs_16_
  37.9 0.0 collective-permute-done.11.refs_17_
  37.9 0.0 collective-permute-done.12.refs_18_
  37.9 4.0 %shard_map.48 = bf16[128,1024]{1,0:T(8,128)(2,1)S(1)} custom-call(bf16[768,1024]{1,0:T(8,128)(2,1)} %refs_0_.8, bf16[768,1024]{1,0:T(8,128)(2,1)} %refs_3_.9, bf16[768,1024]{1,0:T(8,128)(2,1)} %refs_4_.9, bf16[768,1024]{1,0:T(8,128)(2,1)} %refs_3_.9, bf16[768,1024]{1,0:T(8,128)(2,1)} %refs_4_.9, bf16[96,1024]{1,0:T(8,128)(2,1)S(1)} %copy-done.2, ...), custom_call_target="tpu_custom_call" | custom-call | flops 671088640 | bytes 5242880 | tf_op jit(solution)/shard_map/pallas_call | solution.py:151
  41.9 0.5 fusion.28
  42.4 0.6 collective-permute-start.15
  43.0 3.9 %shard_map.49 = bf16[128,1024]{1,0:T(8,128)(2,1)S(1)} custom-call(bf16[768,1024]{1,0:T(8,128)(2,1)} %refs_0_.8, bf16[768,1024]{1,0:T(8,128)(2,1)} %refs_3_.9, bf16[768,1024]{1,0:T(8,128)(2,1)} %refs_4_.9, bf16[768,1024]{1,0:T(8,128)(2,1)} %refs_3_.9, bf16[768,1024]{1,0:T(8,128)(2,1)} %refs_4_.9, bf16[96,1024]{1,0:T(8,128)(2,1)S(1)} %copy-done.2, ...), custom_call_target="tpu_custom_call" | custom-call | flops 671088640 | bytes 5242880 | tf_op jit(solution)/shard_map/pallas_call | solution.py:151
  46.9 0.5 fusion.31
  47.4 1.6 %collective-permute-start.16 = (bf16[128,1024]{1,0:T(8,128)(2,1)S(1)}, bf16[128,1024]{1,0:T(8,128)(2,1)S(1)}, u32[]{:S(2)}, u32[]{:S(2)}) collective-permute-start(bf16[128,1024]{1,0:T(8,128)(2,1)S(1)} %fusion.31), channel_id=1, source_target_pairs={{0,1},{1,0},{2,3},{3,2},{4,5},{5,4},{6,7},{7,6},{8,9},{9,8},{10,11... | collective-permute-start | bytes 786440 | tf_op jit(solution)/shard_map/ppermute | solution.py:258
  48.9 0.4 fusion.34.refs_1_
  49.4 2.1 %collective-permute-done.15.refs_0_ = bf16[128,1024]{1,0:T(8,128)(2,1)S(1)} collective-permute-done((bf16[128,1024]{1,0:T(8,128)(2,1)S(1)}, bf16[128,1024]{1,0:T(8,128)(2,1)S(1)}, u32[]{:S(2)}, u32[]{:S(2)}) %collective-permute-start.15) | collective-permute-done | bytes 262176 | tf_op jit(solution)/shard_map/ppermute | solution.py:258
  51.5 5.8 %shard_map.50 = bf16[256,1024]{1,0:T(8,128)(2,1)S(1)} custom-call(bf16[768,1024]{1,0:T(8,128)(2,1)} %refs_0_.8, bf16[768,1024]{1,0:T(8,128)(2,1)} %refs_3_.9, bf16[768,1024]{1,0:T(8,128)(2,1)} %refs_4_.9, bf16[768,1024]{1,0:T(8,128)(2,1)} %refs_3_.9, bf16[768,1024]{1,0:T(8,128)(2,1)} %refs_4_.9, bf16[96,1024]{1,0:T(8,128)(2,1)S(1)} %copy-done.2, ...), custom_call_target="tpu_custom_call" | custom-call | flops 1342177280 | bytes 5242880 | tf_op jit(solution)/shard_map/pallas_call | solution.py:151
  57.3 0.7 fusion.16
  58.0 0.1 collective-permute-start.19
  58.1 0.0 collective-permute-done.16.refs_0_
  58.1 0.0 collective-permute-done.17.refs_1_.refs_2_
  58.1 0.0 copy-start.5
  58.1 1.0 %copy-done.5 = bf16[512,1024]{1,0:T(8,128)(2,1)} copy-done((bf16[512,1024]{1,0:T(8,128)(2,1)}, bf16[512,1024]{1,0:T(8,128)(2,1)S(1)}, u32[]{:S(2)}) %copy-start.5) | copy-done | bytes 1048600
  59.1 5.8 %shard_map.51 = bf16[256,1024]{1,0:T(8,128)(2,1)S(1)} custom-call(bf16[768,1024]{1,0:T(8,128)(2,1)} %refs_0_.8, bf16[512,1024]{1,0:T(8,128)(2,1)} %copy-done.5, bf16[512,1024]{1,0:T(8,128)(2,1)} %copy-done.5, bf16[768,1024]{1,0:T(8,128)(2,1)} %refs_3_.9, bf16[768,1024]{1,0:T(8,128)(2,1)} %refs_4_.9, bf16[96,1024]{1,0:T(8,128)(2,1)S(1)} %copy-done.2, ...), custom_call_target="tpu_custom_call" | custom-call | flops 1342177280 | bytes 5242880 | tf_op jit(solution)/shard_map/pallas_call | solution.py:151
  64.8 0.7 fusion.19
  65.6 2.1 %collective-permute-start.18 = (bf16[256,1024]{1,0:T(8,128)(2,1)S(1)}, bf16[256,1024]{1,0:T(8,128)(2,1)S(1)}, u32[]{:S(2)}, u32[]{:S(2)}) collective-permute-start(bf16[256,1024]{1,0:T(8,128)(2,1)S(1)} %fusion.19), channel_id=1, source_target_pairs={{0,1},{1,0},{2,3},{3,2},{4,5},{5,4},{6,7},{7,6},{8,9},{9,8},{10,11... | collective-permute-start | bytes 1572872 | tf_op jit(solution)/shard_map/ppermute | solution.py:258
  67.6 0.4 fusion.37.refs_1_
  68.1 0.7 fusion.22.refs_1_
  68.8 0.7 fusion.25.refs_1_
  69.5 0.8 shard_map.52.refs_2_
  70.3 0.8 shard_map.53.refs_2_
  71.1 1.8 %collective-permute-done.19.refs_0_ = bf16[256,1024]{1,0:T(8,128)(2,1)S(1)} collective-permute-done((bf16[256,1024]{1,0:T(8,128)(2,1)S(1)}, bf16[256,1024]{1,0:T(8,128)(2,1)S(1)}, u32[]{:S(2)}, u32[]{:S(2)}) %collective-permute-start.19) | collective-permute-done | bytes 524320 | tf_op jit(solution)/shard_map/ppermute | solution.py:258
  72.9 0.9 %shard_map.54.refs_2_ = bf16[768,1024]{1,0:T(8,128)(2,1)} custom-call(bf16[256,1024]{1,0:T(8,128)(2,1)S(1)} %collective-permute-done.19.refs_0_, bf16[256,1024]{1,0:T(8,128)(2,1)S(1)} %fusion.22.refs_1_, bf16[768,1024]{1,0:T(8,128)(2,1)} %shard_map.53.refs_2_), custom_call_target="tpu_custom_call", output_to_operand_aliasing={{}: (2, {})} | custom-call | bytes 2097152 | tf_op jit(solution)/shard_map/pallas_call | solution.py:177
  73.8 7.6 %collective-permute-done.18.refs_0_ = bf16[256,1024]{1,0:T(8,128)(2,1)S(1)} collective-permute-done((bf16[256,1024]{1,0:T(8,128)(2,1)S(1)}, bf16[256,1024]{1,0:T(8,128)(2,1)S(1)}, u32[]{:S(2)}, u32[]{:S(2)}) %collective-permute-start.18) | collective-permute-done | bytes 524320 | tf_op jit(solution)/shard_map/ppermute | solution.py:258
  81.4 0.9 %shard_map.55 = bf16[768,1024]{1,0:T(8,128)(2,1)} custom-call(bf16[256,1024]{1,0:T(8,128)(2,1)S(1)} %collective-permute-done.18.refs_0_, bf16[256,1024]{1,0:T(8,128)(2,1)S(1)} %fusion.25.refs_1_, bf16[768,1024]{1,0:T(8,128)(2,1)} %shard_map.54.refs_2_), custom_call_target="tpu_custom_call", output_to_operand_aliasing={{}: (2, {})} | custom-call | bytes 2097152 | tf_op jit(solution)/shard_map/pallas_call | solution.py:177
  (6 shorter events, 0.0 us)
Async XLA Ops:
  0.0 14.7 %copy-start = (bf16[768,1024]{1,0:T(8,128)(2,1)S(1)}, bf16[768,1024]{1,0:T(8,128)(2,1)}, u32[]{:S(2)}) copy-start(bf16[768,1024]{1,0:T(8,128)(2,1)} %refs_3_.9) | copy-start | bytes 4718596
  1.6 6.9 %collective-permute-start.1 = (bf16[96,1024]{1,0:T(8,128)(2,1)}, bf16[96,1024]{1,0:T(8,128)(2,1)S(1)}, u32[]{:S(2)}, u32[]{:S(2)}) collective-permute-start(bf16[96,1024]{1,0:T(8,128)(2,1)} %shard_map.46.refs_5_), channel_id=1, source_target_pairs={{0,4},{2,6},{4,0},{6,2},{8,12},{10,14},{12,8},{14,10},{16,20},{18,... | collective-permute-start | bytes 589832 | tf_op jit(solution)/shard_map/ppermute | solution.py:213
  3.2 8.5 %collective-permute-start = (bf16[96,1024]{1,0:T(8,128)(2,1)}, bf16[96,1024]{1,0:T(8,128)(2,1)S(1)}, u32[]{:S(2)}, u32[]{:S(2)}) collective-permute-start(bf16[96,1024]{1,0:T(8,128)(2,1)} %shard_map.46.refs_5_), channel_id=1, source_target_pairs={{0,8},{2,10},{4,12},{6,14},{8,16},{10,18},{12,20},{14,22},{16,24},... | collective-permute-start | bytes 589832 | tf_op jit(solution)/shard_map/ppermute | solution.py:213
  11.6 5.7 %collective-permute-start.3 = (bf16[96,1024]{1,0:T(8,128)(2,1)S(1)}, bf16[96,1024]{1,0:T(8,128)(2,1)S(1)}, u32[]{:S(2)}, u32[]{:S(2)}) collective-permute-start(bf16[96,1024]{1,0:T(8,128)(2,1)S(1)} %collective-permute-done.refs_6_), channel_id=1, source_target_pairs={{0,4},{2,6},{4,0},{6,2},{8,12},{10,14},{12,8},{14,10},{16,20},{18,... | collective-permute-start | bytes 589832 | tf_op jit(solution)/shard_map/ppermute | solution.py:213
  12.1 9.7 %collective-permute-start.2 = (bf16[96,1024]{1,0:T(8,128)(2,1)S(1)}, bf16[96,1024]{1,0:T(8,128)(2,1)S(1)}, u32[]{:S(2)}, u32[]{:S(2)}) collective-permute-start(bf16[96,1024]{1,0:T(8,128)(2,1)S(1)} %collective-permute-done.refs_6_), channel_id=1, source_target_pairs={{8,16},{10,18},{12,20},{14,22},{16,24},{18,26},{20,28},{22,30},{9,... | collective-permute-start | bytes 589832 | tf_op jit(solution)/shard_map/ppermute | solution.py:213
  13.4 14.1 %collective-permute-start.9 = (bf16[96,1024]{1,0:T(8,128)(2,1)}, bf16[96,1024]{1,0:T(8,128)(2,1)S(1)}, u32[]{:S(2)}, u32[]{:S(2)}) collective-permute-start(bf16[96,1024]{1,0:T(8,128)(2,1)} %shard_map.46.refs_5_), channel_id=1, source_target_pairs={{0,28},{2,30},{4,24},{6,26},{1,29},{3,31},{5,25},{7,27}} | collective-permute-start | bytes 589832 | tf_op jit(solution)/shard_map/ppermute | solution.py:213
  14.7 1.4 %copy-start.1 = (bf16[768,1024]{1,0:T(8,128)(2,1)S(1)}, bf16[768,1024]{1,0:T(8,128)(2,1)}, u32[]{:S(2)}) copy-start(bf16[768,1024]{1,0:T(8,128)(2,1)} %refs_4_.9) | copy-start | bytes 4718596
  16.1 17.6 %copy-start.2 = (bf16[96,1024]{1,0:T(8,128)(2,1)S(1)}, bf16[96,1024]{1,0:T(8,128)(2,1)}, u32[]{:S(2)}) copy-start(bf16[96,1024]{1,0:T(8,128)(2,1)} %shard_map.46.refs_5_) | copy-start | bytes 589828
  16.2 1.0 %copy-start.3 = (bf16[512,1024]{1,0:T(8,128)(2,1)}, bf16[512,1024]{1,0:T(8,128)(2,1)S(1)}, u32[]{:S(2)}) copy-start(bf16[512,1024]{1,0:T(8,128)(2,1)S(1)} %shard_map.47) | copy-start | bytes 3145732
  21.8 8.1 %collective-permute-start.8 = (bf16[96,1024]{1,0:T(8,128)(2,1)S(1)}, bf16[96,1024]{1,0:T(8,128)(2,1)S(1)}, u32[]{:S(2)}, u32[]{:S(2)}) collective-permute-start(bf16[96,1024]{1,0:T(8,128)(2,1)S(1)} %collective-permute-done.2.refs_11_), channel_id=1, source_target_pairs={{0,4},{2,6},{4,0},{6,2},{8,12},{10,14},{12,8},{14,10},{16,20},{18,... | collective-permute-start | bytes 589832 | tf_op jit(solution)/shard_map/ppermute | solution.py:213
  26.2 7.6 %collective-permute-start.4 = (bf16[96,1024]{1,0:T(8,128)(2,1)S(1)}, bf16[96,1024]{1,0:T(8,128)(2,1)S(1)}, u32[]{:S(2)}, u32[]{:S(2)}) collective-permute-start(bf16[96,1024]{1,0:T(8,128)(2,1)S(1)} %collective-permute-done.2.refs_11_), channel_id=1, source_target_pairs={{16,24},{18,26},{20,28},{22,30},{17,25},{19,27},{21,29},{23,31}} | collective-permute-start | bytes 589832 | tf_op jit(solution)/shard_map/ppermute | solution.py:213
  27.5 6.8 %collective-permute-start.14 = (bf16[96,1024]{1,0:T(8,128)(2,1)S(1)}, bf16[96,1024]{1,0:T(8,128)(2,1)S(1)}, u32[]{:S(2)}, u32[]{:S(2)}) collective-permute-start(bf16[96,1024]{1,0:T(8,128)(2,1)S(1)} %collective-permute-done.9.refs_15_), channel_id=1, source_target_pairs={{0,2},{2,0},{4,6},{6,4},{8,10},{10,8},{12,14},{14,12},{16,18},{18,... | collective-permute-start | bytes 589832 | tf_op jit(solution)/shard_map/ppermute | solution.py:213
  29.9 4.9 %collective-permute-start.13 = (bf16[96,1024]{1,0:T(8,128)(2,1)S(1)}, bf16[96,1024]{1,0:T(8,128)(2,1)S(1)}, u32[]{:S(2)}, u32[]{:S(2)}) collective-permute-start(bf16[96,1024]{1,0:T(8,128)(2,1)S(1)} %collective-permute-done.8.refs_14_), channel_id=1, source_target_pairs={{0,2},{2,0},{4,6},{6,4},{8,10},{10,8},{12,14},{14,12},{16,18},{18,... | collective-permute-start | bytes 589832 | tf_op jit(solution)/shard_map/ppermute | solution.py:213
  33.8 1.4 %collective-permute-start.5 = (bf16[96,1024]{1,0:T(8,128)(2,1)S(1)}, bf16[96,1024]{1,0:T(8,128)(2,1)S(1)}, u32[]{:S(2)}, u32[]{:S(2)}) collective-permute-start(bf16[96,1024]{1,0:T(8,128)(2,1)S(1)} %copy-done.2), channel_id=1, source_target_pairs={{0,2},{2,0},{4,6},{6,4},{8,10},{10,8},{12,14},{14,12},{16,18},{18,... | collective-permute-start | bytes 589832 | tf_op jit(solution)/shard_map/ppermute | solution.py:213
  33.8 1.7 %collective-permute-start.6 = (bf16[96,1024]{1,0:T(8,128)(2,1)S(1)}, bf16[96,1024]{1,0:T(8,128)(2,1)S(1)}, u32[]{:S(2)}, u32[]{:S(2)}) collective-permute-start(bf16[96,1024]{1,0:T(8,128)(2,1)S(1)} %collective-permute-done.refs_6_), channel_id=1, source_target_pairs={{0,2},{2,0},{4,6},{6,4},{8,10},{10,8},{12,14},{14,12},{16,18},{18,... | collective-permute-start | bytes 589832 | tf_op jit(solution)/shard_map/ppermute | solution.py:213
  34.3 3.6 %collective-permute-start.7 = (bf16[96,1024]{1,0:T(8,128)(2,1)S(1)}, bf16[96,1024]{1,0:T(8,128)(2,1)S(1)}, u32[]{:S(2)}, u32[]{:S(2)}) collective-permute-start(bf16[96,1024]{1,0:T(8,128)(2,1)S(1)} %collective-permute-done.1.refs_7_), channel_id=1, source_target_pairs={{0,2},{2,0},{4,6},{6,4},{8,10},{10,8},{12,14},{14,12},{16,18},{18,... | collective-permute-start | bytes 589832 | tf_op jit(solution)/shard_map/ppermute | solution.py:213
  34.3 3.6 %collective-permute-start.10 = (bf16[96,1024]{1,0:T(8,128)(2,1)S(1)}, bf16[96,1024]{1,0:T(8,128)(2,1)S(1)}, u32[]{:S(2)}, u32[]{:S(2)}) collective-permute-start(bf16[96,1024]{1,0:T(8,128)(2,1)S(1)} %collective-permute-done.2.refs_11_), channel_id=1, source_target_pairs={{0,2},{2,0},{4,6},{6,4},{8,10},{10,8},{12,14},{14,12},{16,18},{18,... | collective-permute-start | bytes 589832 | tf_op jit(solution)/shard_map/ppermute | solution.py:213
  34.8 3.1 %collective-permute-start.11 = (bf16[96,1024]{1,0:T(8,128)(2,1)S(1)}, bf16[96,1024]{1,0:T(8,128)(2,1)S(1)}, u32[]{:S(2)}, u32[]{:S(2)}) collective-permute-start(bf16[96,1024]{1,0:T(8,128)(2,1)S(1)} %collective-permute-done.3.refs_12_), channel_id=1, source_target_pairs={{0,2},{2,0},{4,6},{6,4},{8,10},{10,8},{12,14},{14,12},{16,18},{18,... | collective-permute-start | bytes 589832 | tf_op jit(solution)/shard_map/ppermute | solution.py:213
  35.2 2.7 %collective-permute-start.12 = (bf16[96,1024]{1,0:T(8,128)(2,1)S(1)}, bf16[96,1024]{1,0:T(8,128)(2,1)S(1)}, u32[]{:S(2)}, u32[]{:S(2)}) collective-permute-start(bf16[96,1024]{1,0:T(8,128)(2,1)S(1)} %collective-permute-done.4.refs_13_), channel_id=1, source_target_pairs={{0,2},{2,0},{4,6},{6,4},{8,10},{10,8},{12,14},{14,12},{16,18},{18,... | collective-permute-start | bytes 589832 | tf_op jit(solution)/shard_map/ppermute | solution.py:213
  35.3 6.5 %copy-start.4 = (bf16[1024,2048]{1,0:T(8,128)(2,1)S(1)}, bf16[1024,2048]{1,0:T(8,128)(2,1)}, u32[]{:S(2)}) copy-start(bf16[1024,2048]{1,0:T(8,128)(2,1)} %param.7) | copy-start | bytes 12582916
  35.5 22.6 %collective-permute-start.17 = (bf16[512,1024]{1,0:T(8,128)(2,1)}, bf16[512,1024]{1,0:T(8,128)(2,1)S(1)}, u32[]{:S(2)}, u32[]{:S(2)}) collective-permute-start(bf16[512,1024]{1,0:T(8,128)(2,1)} %copy-done.3), channel_id=1, source_target_pairs={{0,2},{2,4},{4,6},{6,8},{8,10},{10,12},{12,14},{14,16},{16,18},{18... | collective-permute-start | bytes 3145736 | tf_op jit(solution)/shard_map/ppermute | solution.py:233
  42.4 9.1 %collective-permute-start.15 = (bf16[128,1024]{1,0:T(8,128)(2,1)S(1)}, bf16[128,1024]{1,0:T(8,128)(2,1)S(1)}, u32[]{:S(2)}, u32[]{:S(2)}) collective-permute-start(bf16[128,1024]{1,0:T(8,128)(2,1)S(1)} %fusion.28), channel_id=1, source_target_pairs={{0,1},{1,0},{2,3},{3,2},{4,5},{5,4},{6,7},{7,6},{8,9},{9,8},{10,11... | collective-permute-start | bytes 786440 | tf_op jit(solution)/shard_map/ppermute | solution.py:258
  47.4 10.7 %collective-permute-start.16 = (bf16[128,1024]{1,0:T(8,128)(2,1)S(1)}, bf16[128,1024]{1,0:T(8,128)(2,1)S(1)}, u32[]{:S(2)}, u32[]{:S(2)}) collective-permute-start(bf16[128,1024]{1,0:T(8,128)(2,1)S(1)} %fusion.31), channel_id=1, source_target_pairs={{0,1},{1,0},{2,3},{3,2},{4,5},{5,4},{6,7},{7,6},{8,9},{9,8},{10,11... | collective-permute-start | bytes 786440 | tf_op jit(solution)/shard_map/ppermute | solution.py:258
  58.0 14.9 %collective-permute-start.19 = (bf16[256,1024]{1,0:T(8,128)(2,1)S(1)}, bf16[256,1024]{1,0:T(8,128)(2,1)S(1)}, u32[]{:S(2)}, u32[]{:S(2)}) collective-permute-start(bf16[256,1024]{1,0:T(8,128)(2,1)S(1)} %fusion.16), channel_id=1, source_target_pairs={{0,1},{1,0},{2,3},{3,2},{4,5},{5,4},{6,7},{7,6},{8,9},{9,8},{10,11... | collective-permute-start | bytes 1572872 | tf_op jit(solution)/shard_map/ppermute | solution.py:258
  58.1 1.0 %copy-start.5 = (bf16[512,1024]{1,0:T(8,128)(2,1)}, bf16[512,1024]{1,0:T(8,128)(2,1)S(1)}, u32[]{:S(2)}) copy-start(bf16[512,1024]{1,0:T(8,128)(2,1)S(1)} %collective-permute-done.17.refs_1_.refs_2_) | copy-start | bytes 3145732
  65.6 15.9 %collective-permute-start.18 = (bf16[256,1024]{1,0:T(8,128)(2,1)S(1)}, bf16[256,1024]{1,0:T(8,128)(2,1)S(1)}, u32[]{:S(2)}, u32[]{:S(2)}) collective-permute-start(bf16[256,1024]{1,0:T(8,128)(2,1)S(1)} %fusion.19), channel_id=1, source_target_pairs={{0,1},{1,0},{2,3},{3,2},{4,5},{5,4},{6,7},{7,6},{8,9},{9,8},{10,11... | collective-permute-start | bytes 1572872 | tf_op jit(solution)/shard_map/ppermute | solution.py:258

commit v4 on v3

--- a/solution.py
+++ b/solution.py
@@ -224,7 +224,8 @@
         z2, y1 = up(z1, 2), flip(z1, 2)
         z2, y1, tail = tie((z2, y1, tail_rows(keys, values)))
         z3, y2 = up(z2, 3), flip(z2, 2)
-        z3, tail, own, z1, y0, z2, y1 = tie((z3, tail, own, z1, y0, z2, y1))
+        y2, tail, z2, y1 = tie((y2, tail, z2, y1))
+        z3, own, z1, y0 = tie((z3, own, z1, y0))
         early = {(0, 0, 0): own, (1, 0, 0): z1, (0, 1, 0): y0}
         late = {(2, 0, 0): z2, (1, 1, 0): y1, (3, 0, 0): z3, (2, 1, 0): y2, (3, 1, 0): far}
         early |= {(k, y, 1): flip(p, 1) for (k, y, _), p in list(early.items())}

time: 82.7 us -> 81.9 us (level)
  waiting for transfers between devices: 30 us -> 29.1 us
    ppermute x15, waiting for transfers between devices: 18.4 us -> 17.4 us  [send(): return lax.ppermute(value, 'ctx', pairs)]
  transfers between devices with their start and end apart: 20 -> 20, of which waited for: 11 -> 9; matrix products, arithmetic and copies ran while one was open for 6% -> 6% of each run, Pallas kernels for 27% -> 27%
where the time goes in v4:
time: 81.9 us; the launch traced here: 81.6 us
  waiting for transfers between devices  29.1 us (36%)
  Pallas kernels  24.5 us (30%)
  starting transfers between devices  19.7 us (24%)
  matrix products  4.67 us (6%)
  local copies, waits for them, and re-layouts  3.34 us (4%)
    pallas_call x4, Pallas kernels, attend(): pl.pallas_call(functools.partial(attend_kernel, cfg), grid=(steps,), in_s...  19.4 us
    ppermute x15, waiting for transfers between devices, send(): return lax.ppermute(value, 'ctx', pairs)  17.4 us
    ppermute x15, starting transfers between devices, send(): return lax.ppermute(value, 'ctx', pairs)  13.2 us
    ppermute x4, waiting for transfers between devices, per_device(): lax.ppermute(value, 'head', [(i, (i + step) % n_head) for i in range(n_he...  11.7 us
    dot_general x8, matrix products, partial(): jnp.dot(att, w, preferred_element_type=jnp.float32).astype(jnp.bfloat16)  4.67 us
    ppermute x4, starting transfers between devices, per_device(): lax.ppermute(value, 'head', [(i, (i + step) % n_head) for i in range(n_he...  4.29 us
    pallas_call x4, Pallas kernels, add_into(): pl.pallas_call(functools.partial(add_kernel, len(parts)), grid=(1,), in_s...  3.36 us
    unnamed x12, local copies, waits for them, and re-layouts  3.34 us
  transfers between devices with their start and end apart: 20, of which 9 were waited for; matrix products, arithmetic and copies ran while one was open for 6% of the time, Pallas kernels for 27%

profile of v4, /device:TPU:26, one launch (start us, length us, event | category | flops | bytes accessed | tf_op | source)
XLA Modules:
  0.0 81.6 jit_solution(9441079991487020380)
XLA Ops:
  0.0 1.6 %shard_map.46.refs_5_ = bf16[96,1024]{1,0:T(8,128)(2,1)} custom-call(bf16[768,1024]{1,0:T(8,128)(2,1)} %refs_3_.9, bf16[768,1024]{1,0:T(8,128)(2,1)} %refs_3_.9, bf16[768,1024]{1,0:T(8,128)(2,1)} %refs_3_.9, bf16[768,1024]{1,0:T(8,128)(2,1)} %refs_4_.9, bf16[768,1024]{1,0:T(8,128)(2,1)} %refs_4_.9, bf16[768,1024]{1,0:T(8,128)(2,1)} %refs_4_.9), custom_call_target="tpu_custom_call" | custom-call | bytes 393216 | tf_op jit(solution)/shard_map/pallas_call | solution.py:30
  1.6 1.5 %collective-permute-start.1 = (bf16[96,1024]{1,0:T(8,128)(2,1)}, bf16[96,1024]{1,0:T(8,128)(2,1)S(1)}, u32[]{:S(2)}, u32[]{:S(2)}) collective-permute-start(bf16[96,1024]{1,0:T(8,128)(2,1)} %shard_map.46.refs_5_), channel_id=1, source_target_pairs={{0,4},{2,6},{4,0},{6,2},{8,12},{10,14},{12,8},{14,10},{16,20},{18,... | collective-permute-start | bytes 589832 | tf_op jit(solution)/shard_map/ppermute | solution.py:213
  3.2 1.3 %collective-permute-start = (bf16[96,1024]{1,0:T(8,128)(2,1)}, bf16[96,1024]{1,0:T(8,128)(2,1)S(1)}, u32[]{:S(2)}, u32[]{:S(2)}) collective-permute-start(bf16[96,1024]{1,0:T(8,128)(2,1)} %shard_map.46.refs_5_), channel_id=1, source_target_pairs={{0,8},{2,10},{4,12},{6,14},{8,16},{10,18},{12,20},{14,22},{16,24},... | collective-permute-start | bytes 589832 | tf_op jit(solution)/shard_map/ppermute | solution.py:213
  4.5 4.0 %collective-permute-done.1.refs_7_ = bf16[96,1024]{1,0:T(8,128)(2,1)S(1)} collective-permute-done((bf16[96,1024]{1,0:T(8,128)(2,1)}, bf16[96,1024]{1,0:T(8,128)(2,1)S(1)}, u32[]{:S(2)}, u32[]{:S(2)}) %collective-permute-start.1) | collective-permute-done | bytes 196640 | tf_op jit(solution)/shard_map/ppermute | solution.py:213
  8.5 3.1 %collective-permute-done.refs_6_ = bf16[96,1024]{1,0:T(8,128)(2,1)S(1)} collective-permute-done((bf16[96,1024]{1,0:T(8,128)(2,1)}, bf16[96,1024]{1,0:T(8,128)(2,1)S(1)}, u32[]{:S(2)}, u32[]{:S(2)}) %collective-permute-start) | collective-permute-done | bytes 196640 | tf_op jit(solution)/shard_map/ppermute | solution.py:213
  11.6 0.5 collective-permute-start.3
  12.1 1.3 %collective-permute-start.2 = (bf16[96,1024]{1,0:T(8,128)(2,1)S(1)}, bf16[96,1024]{1,0:T(8,128)(2,1)S(1)}, u32[]{:S(2)}, u32[]{:S(2)}) collective-permute-start(bf16[96,1024]{1,0:T(8,128)(2,1)S(1)} %collective-permute-done.refs_6_), channel_id=1, source_target_pairs={{8,16},{10,18},{12,20},{14,22},{16,24},{18,26},{20,28},{22,30},{9,... | collective-permute-start | bytes 589832 | tf_op jit(solution)/shard_map/ppermute | solution.py:213
  13.4 1.3 %collective-permute-start.9 = (bf16[96,1024]{1,0:T(8,128)(2,1)}, bf16[96,1024]{1,0:T(8,128)(2,1)S(1)}, u32[]{:S(2)}, u32[]{:S(2)}) collective-permute-start(bf16[96,1024]{1,0:T(8,128)(2,1)} %shard_map.46.refs_5_), channel_id=1, source_target_pairs={{0,28},{2,30},{4,24},{6,26},{1,29},{3,31},{5,25},{7,27}} | collective-permute-start | bytes 589832 | tf_op jit(solution)/shard_map/ppermute | solution.py:213
  14.7 0.0 copy-start.1
  14.7 1.4 %copy-done.1 = bf16[768,1024]{1,0:T(8,128)(2,1)S(1)} copy-done((bf16[768,1024]{1,0:T(8,128)(2,1)S(1)}, bf16[768,1024]{1,0:T(8,128)(2,1)}, u32[]{:S(2)}) %copy-start.1) | copy-done | bytes 1572888
  16.1 0.1 shard_map.47
  16.2 0.0 copy-start.3
  16.2 1.0 %copy-done.3 = bf16[512,1024]{1,0:T(8,128)(2,1)} copy-done((bf16[512,1024]{1,0:T(8,128)(2,1)}, bf16[512,1024]{1,0:T(8,128)(2,1)S(1)}, u32[]{:S(2)}) %copy-start.3) | copy-done | bytes 1048600
  17.2 0.1 collective-permute-done.3.refs_12_
  17.3 4.5 %collective-permute-done.2.refs_11_ = bf16[96,1024]{1,0:T(8,128)(2,1)S(1)} collective-permute-done((bf16[96,1024]{1,0:T(8,128)(2,1)S(1)}, bf16[96,1024]{1,0:T(8,128)(2,1)S(1)}, u32[]{:S(2)}, u32[]{:S(2)}) %collective-permute-start.2) | collective-permute-done | bytes 196640 | tf_op jit(solution)/shard_map/ppermute | solution.py:213
  21.8 4.4 %collective-permute-start.8 = (bf16[96,1024]{1,0:T(8,128)(2,1)S(1)}, bf16[96,1024]{1,0:T(8,128)(2,1)S(1)}, u32[]{:S(2)}, u32[]{:S(2)}) collective-permute-start(bf16[96,1024]{1,0:T(8,128)(2,1)S(1)} %collective-permute-done.2.refs_11_), channel_id=1, source_target_pairs={{0,4},{2,6},{4,0},{6,2},{8,12},{10,14},{12,8},{14,10},{16,20},{18,... | collective-permute-start | bytes 589832 | tf_op jit(solution)/shard_map/ppermute | solution.py:213
  26.2 1.3 %collective-permute-start.4 = (bf16[96,1024]{1,0:T(8,128)(2,1)S(1)}, bf16[96,1024]{1,0:T(8,128)(2,1)S(1)}, u32[]{:S(2)}, u32[]{:S(2)}) collective-permute-start(bf16[96,1024]{1,0:T(8,128)(2,1)S(1)} %collective-permute-done.2.refs_11_), channel_id=1, source_target_pairs={{16,24},{18,26},{20,28},{22,30},{17,25},{19,27},{21,29},{23,31}} | collective-permute-start | bytes 589832 | tf_op jit(solution)/shard_map/ppermute | solution.py:213
  27.5 0.0 collective-permute-done.9.refs_15_
  27.5 0.1 collective-permute-start.14
  27.6 2.3 %collective-permute-done.8.refs_14_ = bf16[96,1024]{1,0:T(8,128)(2,1)S(1)} collective-permute-done((bf16[96,1024]{1,0:T(8,128)(2,1)S(1)}, bf16[96,1024]{1,0:T(8,128)(2,1)S(1)}, u32[]{:S(2)}, u32[]{:S(2)}) %collective-permute-start.8) | collective-permute-done | bytes 196640 | tf_op jit(solution)/shard_map/ppermute | solution.py:213
  29.9 0.0 collective-permute-start.10
  29.9 0.5 collective-permute-start.11
  30.4 0.0 collective-permute-start.13
  30.4 3.4 %collective-permute-done.4.refs_13_ = bf16[96,1024]{1,0:T(8,128)(2,1)S(1)} collective-permute-done((bf16[96,1024]{1,0:T(8,128)(2,1)S(1)}, bf16[96,1024]{1,0:T(8,128)(2,1)S(1)}, u32[]{:S(2)}, u32[]{:S(2)}) %collective-permute-start.4) | collective-permute-done | bytes 196640 | tf_op jit(solution)/shard_map/ppermute | solution.py:213
  33.8 0.0 collective-permute-start.5
  33.8 0.0 collective-permute-done.14.refs_20_
  33.8 0.5 collective-permute-start.6
  34.3 0.0 collective-permute-done.10.refs_16_
  34.3 0.1 collective-permute-start.7
  34.4 0.0 collective-permute-done.11.refs_17_
  34.4 0.4 collective-permute-start.12
  34.8 0.0 collective-permute-done.13.refs_19_
  34.8 2.2 %collective-permute-start.17 = (bf16[512,1024]{1,0:T(8,128)(2,1)}, bf16[512,1024]{1,0:T(8,128)(2,1)S(1)}, u32[]{:S(2)}, u32[]{:S(2)}) collective-permute-start(bf16[512,1024]{1,0:T(8,128)(2,1)} %copy-done.3), channel_id=1, source_target_pairs={{0,2},{2,4},{4,6},{6,8},{8,10},{10,12},{12,14},{14,16},{16,18},{18... | collective-permute-start | bytes 3145736 | tf_op jit(solution)/shard_map/ppermute | solution.py:234
  37.0 0.0 collective-permute-done.5.refs_8_
  37.0 0.0 collective-permute-done.6.refs_9_
  37.1 0.0 collective-permute-done.7.refs_10_
  37.1 0.0 collective-permute-done.12.refs_18_
  37.1 4.0 %shard_map.48 = bf16[128,1024]{1,0:T(8,128)(2,1)S(1)} custom-call(bf16[768,1024]{1,0:T(8,128)(2,1)} %refs_0_.8, bf16[768,1024]{1,0:T(8,128)(2,1)} %refs_3_.9, bf16[768,1024]{1,0:T(8,128)(2,1)} %refs_4_.9, bf16[768,1024]{1,0:T(8,128)(2,1)} %refs_3_.9, bf16[768,1024]{1,0:T(8,128)(2,1)} %refs_4_.9, bf16[96,1024]{1,0:T(8,128)(2,1)S(1)} %copy-done.2, ...), custom_call_target="tpu_custom_call" | custom-call | flops 671088640 | bytes 5242880 | tf_op jit(solution)/shard_map/pallas_call | solution.py:151
  41.0 0.5 fusion.28
  41.5 0.6 collective-permute-start.15
  42.1 3.9 %shard_map.49 = bf16[128,1024]{1,0:T(8,128)(2,1)S(1)} custom-call(bf16[768,1024]{1,0:T(8,128)(2,1)} %refs_0_.8, bf16[768,1024]{1,0:T(8,128)(2,1)} %refs_3_.9, bf16[768,1024]{1,0:T(8,128)(2,1)} %refs_4_.9, bf16[768,1024]{1,0:T(8,128)(2,1)} %refs_3_.9, bf16[768,1024]{1,0:T(8,128)(2,1)} %refs_4_.9, bf16[96,1024]{1,0:T(8,128)(2,1)S(1)} %copy-done.2, ...), custom_call_target="tpu_custom_call" | custom-call | flops 671088640 | bytes 5242880 | tf_op jit(solution)/shard_map/pallas_call | solution.py:151
  46.0 0.5 fusion.31
  46.5 1.6 %collective-permute-start.16 = (bf16[128,1024]{1,0:T(8,128)(2,1)S(1)}, bf16[128,1024]{1,0:T(8,128)(2,1)S(1)}, u32[]{:S(2)}, u32[]{:S(2)}) collective-permute-start(bf16[128,1024]{1,0:T(8,128)(2,1)S(1)} %fusion.31), channel_id=1, source_target_pairs={{0,1},{1,0},{2,3},{3,2},{4,5},{5,4},{6,7},{7,6},{8,9},{9,8},{10,11... | collective-permute-start | bytes 786440 | tf_op jit(solution)/shard_map/ppermute | solution.py:259
  48.1 0.4 fusion.34.refs_1_
  48.5 2.2 %collective-permute-done.15.refs_0_ = bf16[128,1024]{1,0:T(8,128)(2,1)S(1)} collective-permute-done((bf16[128,1024]{1,0:T(8,128)(2,1)S(1)}, bf16[128,1024]{1,0:T(8,128)(2,1)S(1)}, u32[]{:S(2)}, u32[]{:S(2)}) %collective-permute-start.15) | collective-permute-done | bytes 262176 | tf_op jit(solution)/shard_map/ppermute | solution.py:259
  50.7 5.8 %shard_map.50 = bf16[256,1024]{1,0:T(8,128)(2,1)S(1)} custom-call(bf16[768,1024]{1,0:T(8,128)(2,1)} %refs_0_.8, bf16[768,1024]{1,0:T(8,128)(2,1)} %refs_3_.9, bf16[768,1024]{1,0:T(8,128)(2,1)} %refs_4_.9, bf16[768,1024]{1,0:T(8,128)(2,1)} %refs_3_.9, bf16[768,1024]{1,0:T(8,128)(2,1)} %refs_4_.9, bf16[96,1024]{1,0:T(8,128)(2,1)S(1)} %copy-done.2, ...), custom_call_target="tpu_custom_call" | custom-call | flops 1342177280 | bytes 5242880 | tf_op jit(solution)/shard_map/pallas_call | solution.py:151
  56.4 0.7 fusion.16
  57.2 0.1 collective-permute-start.19
  57.2 0.0 collective-permute-done.16.refs_0_
  57.2 0.0 collective-permute-done.17.refs_1_.refs_2_
  57.3 0.0 copy-start.5
  57.3 1.0 %copy-done.5 = bf16[512,1024]{1,0:T(8,128)(2,1)} copy-done((bf16[512,1024]{1,0:T(8,128)(2,1)}, bf16[512,1024]{1,0:T(8,128)(2,1)S(1)}, u32[]{:S(2)}) %copy-start.5) | copy-done | bytes 1048600
  58.2 5.8 %shard_map.51 = bf16[256,1024]{1,0:T(8,128)(2,1)S(1)} custom-call(bf16[768,1024]{1,0:T(8,128)(2,1)} %refs_0_.8, bf16[512,1024]{1,0:T(8,128)(2,1)} %copy-done.5, bf16[512,1024]{1,0:T(8,128)(2,1)} %copy-done.5, bf16[768,1024]{1,0:T(8,128)(2,1)} %refs_3_.9, bf16[768,1024]{1,0:T(8,128)(2,1)} %refs_4_.9, bf16[96,1024]{1,0:T(8,128)(2,1)S(1)} %copy-done.2, ...), custom_call_target="tpu_custom_call" | custom-call | flops 1342177280 | bytes 5242880 | tf_op jit(solution)/shard_map/pallas_call | solution.py:151
  64.0 0.7 fusion.19
  64.7 2.1 %collective-permute-start.18 = (bf16[256,1024]{1,0:T(8,128)(2,1)S(1)}, bf16[256,1024]{1,0:T(8,128)(2,1)S(1)}, u32[]{:S(2)}, u32[]{:S(2)}) collective-permute-start(bf16[256,1024]{1,0:T(8,128)(2,1)S(1)} %fusion.19), channel_id=1, source_target_pairs={{0,1},{1,0},{2,3},{3,2},{4,5},{5,4},{6,7},{7,6},{8,9},{9,8},{10,11... | collective-permute-start | bytes 1572872 | tf_op jit(solution)/shard_map/ppermute | solution.py:259
  66.8 0.4 fusion.37.refs_1_
  67.3 0.7 fusion.22.refs_1_
  68.0 0.7 fusion.25.refs_1_
  68.7 0.8 shard_map.52.refs_2_
  69.5 0.8 shard_map.53.refs_2_
  70.2 1.8 %collective-permute-done.19.refs_0_ = bf16[256,1024]{1,0:T(8,128)(2,1)S(1)} collective-permute-done((bf16[256,1024]{1,0:T(8,128)(2,1)S(1)}, bf16[256,1024]{1,0:T(8,128)(2,1)S(1)}, u32[]{:S(2)}, u32[]{:S(2)}) %collective-permute-start.19) | collective-permute-done | bytes 524320 | tf_op jit(solution)/shard_map/ppermute | solution.py:259
  72.1 0.9 %shard_map.54.refs_2_ = bf16[768,1024]{1,0:T(8,128)(2,1)} custom-call(bf16[256,1024]{1,0:T(8,128)(2,1)S(1)} %collective-permute-done.19.refs_0_, bf16[256,1024]{1,0:T(8,128)(2,1)S(1)} %fusion.22.refs_1_, bf16[768,1024]{1,0:T(8,128)(2,1)} %shard_map.53.refs_2_), custom_call_target="tpu_custom_call", output_to_operand_aliasing={{}: (2, {})} | custom-call | bytes 2097152 | tf_op jit(solution)/shard_map/pallas_call | solution.py:177
  73.0 7.7 %collective-permute-done.18.refs_0_ = bf16[256,1024]{1,0:T(8,128)(2,1)S(1)} collective-permute-done((bf16[256,1024]{1,0:T(8,128)(2,1)S(1)}, bf16[256,1024]{1,0:T(8,128)(2,1)S(1)}, u32[]{:S(2)}, u32[]{:S(2)}) %collective-permute-start.18) | collective-permute-done | bytes 524320 | tf_op jit(solution)/shard_map/ppermute | solution.py:259
  80.7 0.9 %shard_map.55 = bf16[768,1024]{1,0:T(8,128)(2,1)} custom-call(bf16[256,1024]{1,0:T(8,128)(2,1)S(1)} %collective-permute-done.18.refs_0_, bf16[256,1024]{1,0:T(8,128)(2,1)S(1)} %fusion.25.refs_1_, bf16[768,1024]{1,0:T(8,128)(2,1)} %shard_map.54.refs_2_), custom_call_target="tpu_custom_call", output_to_operand_aliasing={{}: (2, {})} | custom-call | bytes 2097152 | tf_op jit(solution)/shard_map/pallas_call | solution.py:177
  (6 shorter events, 0.0 us)
Async XLA Ops:
  0.0 14.7 %copy-start = (bf16[768,1024]{1,0:T(8,128)(2,1)S(1)}, bf16[768,1024]{1,0:T(8,128)(2,1)}, u32[]{:S(2)}) copy-start(bf16[768,1024]{1,0:T(8,128)(2,1)} %refs_3_.9) | copy-start | bytes 4718596
  1.6 6.9 %collective-permute-start.1 = (bf16[96,1024]{1,0:T(8,128)(2,1)}, bf16[96,1024]{1,0:T(8,128)(2,1)S(1)}, u32[]{:S(2)}, u32[]{:S(2)}) collective-permute-start(bf16[96,1024]{1,0:T(8,128)(2,1)} %shard_map.46.refs_5_), channel_id=1, source_target_pairs={{0,4},{2,6},{4,0},{6,2},{8,12},{10,14},{12,8},{14,10},{16,20},{18,... | collective-permute-start | bytes 589832 | tf_op jit(solution)/shard_map/ppermute | solution.py:213
  3.2 8.5 %collective-permute-start = (bf16[96,1024]{1,0:T(8,128)(2,1)}, bf16[96,1024]{1,0:T(8,128)(2,1)S(1)}, u32[]{:S(2)}, u32[]{:S(2)}) collective-permute-start(bf16[96,1024]{1,0:T(8,128)(2,1)} %shard_map.46.refs_5_), channel_id=1, source_target_pairs={{0,8},{2,10},{4,12},{6,14},{8,16},{10,18},{12,20},{14,22},{16,24},... | collective-permute-start | bytes 589832 | tf_op jit(solution)/shard_map/ppermute | solution.py:213
  11.6 5.7 %collective-permute-start.3 = (bf16[96,1024]{1,0:T(8,128)(2,1)S(1)}, bf16[96,1024]{1,0:T(8,128)(2,1)S(1)}, u32[]{:S(2)}, u32[]{:S(2)}) collective-permute-start(bf16[96,1024]{1,0:T(8,128)(2,1)S(1)} %collective-permute-done.refs_6_), channel_id=1, source_target_pairs={{0,4},{2,6},{4,0},{6,2},{8,12},{10,14},{12,8},{14,10},{16,20},{18,... | collective-permute-start | bytes 589832 | tf_op jit(solution)/shard_map/ppermute | solution.py:213
  12.1 9.7 %collective-permute-start.2 = (bf16[96,1024]{1,0:T(8,128)(2,1)S(1)}, bf16[96,1024]{1,0:T(8,128)(2,1)S(1)}, u32[]{:S(2)}, u32[]{:S(2)}) collective-permute-start(bf16[96,1024]{1,0:T(8,128)(2,1)S(1)} %collective-permute-done.refs_6_), channel_id=1, source_target_pairs={{8,16},{10,18},{12,20},{14,22},{16,24},{18,26},{20,28},{22,30},{9,... | collective-permute-start | bytes 589832 | tf_op jit(solution)/shard_map/ppermute | solution.py:213
  13.4 14.1 %collective-permute-start.9 = (bf16[96,1024]{1,0:T(8,128)(2,1)}, bf16[96,1024]{1,0:T(8,128)(2,1)S(1)}, u32[]{:S(2)}, u32[]{:S(2)}) collective-permute-start(bf16[96,1024]{1,0:T(8,128)(2,1)} %shard_map.46.refs_5_), channel_id=1, source_target_pairs={{0,28},{2,30},{4,24},{6,26},{1,29},{3,31},{5,25},{7,27}} | collective-permute-start | bytes 589832 | tf_op jit(solution)/shard_map/ppermute | solution.py:213
  14.7 1.4 %copy-start.1 = (bf16[768,1024]{1,0:T(8,128)(2,1)S(1)}, bf16[768,1024]{1,0:T(8,128)(2,1)}, u32[]{:S(2)}) copy-start(bf16[768,1024]{1,0:T(8,128)(2,1)} %refs_4_.9) | copy-start | bytes 4718596
  16.1 17.6 %copy-start.2 = (bf16[96,1024]{1,0:T(8,128)(2,1)S(1)}, bf16[96,1024]{1,0:T(8,128)(2,1)}, u32[]{:S(2)}) copy-start(bf16[96,1024]{1,0:T(8,128)(2,1)} %shard_map.46.refs_5_) | copy-start | bytes 589828
  16.2 1.0 %copy-start.3 = (bf16[512,1024]{1,0:T(8,128)(2,1)}, bf16[512,1024]{1,0:T(8,128)(2,1)S(1)}, u32[]{:S(2)}) copy-start(bf16[512,1024]{1,0:T(8,128)(2,1)S(1)} %shard_map.47) | copy-start | bytes 3145732
  21.8 8.1 %collective-permute-start.8 = (bf16[96,1024]{1,0:T(8,128)(2,1)S(1)}, bf16[96,1024]{1,0:T(8,128)(2,1)S(1)}, u32[]{:S(2)}, u32[]{:S(2)}) collective-permute-start(bf16[96,1024]{1,0:T(8,128)(2,1)S(1)} %collective-permute-done.2.refs_11_), channel_id=1, source_target_pairs={{0,4},{2,6},{4,0},{6,2},{8,12},{10,14},{12,8},{14,10},{16,20},{18,... | collective-permute-start | bytes 589832 | tf_op jit(solution)/shard_map/ppermute | solution.py:213
  26.2 7.6 %collective-permute-start.4 = (bf16[96,1024]{1,0:T(8,128)(2,1)S(1)}, bf16[96,1024]{1,0:T(8,128)(2,1)S(1)}, u32[]{:S(2)}, u32[]{:S(2)}) collective-permute-start(bf16[96,1024]{1,0:T(8,128)(2,1)S(1)} %collective-permute-done.2.refs_11_), channel_id=1, source_target_pairs={{16,24},{18,26},{20,28},{22,30},{17,25},{19,27},{21,29},{23,31}} | collective-permute-start | bytes 589832 | tf_op jit(solution)/shard_map/ppermute | solution.py:213
  27.5 6.3 %collective-permute-start.14 = (bf16[96,1024]{1,0:T(8,128)(2,1)S(1)}, bf16[96,1024]{1,0:T(8,128)(2,1)S(1)}, u32[]{:S(2)}, u32[]{:S(2)}) collective-permute-start(bf16[96,1024]{1,0:T(8,128)(2,1)S(1)} %collective-permute-done.9.refs_15_), channel_id=1, source_target_pairs={{0,2},{2,0},{4,6},{6,4},{8,10},{10,8},{12,14},{14,12},{16,18},{18,... | collective-permute-start | bytes 589832 | tf_op jit(solution)/shard_map/ppermute | solution.py:213
  29.9 4.4 %collective-permute-start.10 = (bf16[96,1024]{1,0:T(8,128)(2,1)S(1)}, bf16[96,1024]{1,0:T(8,128)(2,1)S(1)}, u32[]{:S(2)}, u32[]{:S(2)}) collective-permute-start(bf16[96,1024]{1,0:T(8,128)(2,1)S(1)} %collective-permute-done.2.refs_11_), channel_id=1, source_target_pairs={{0,2},{2,0},{4,6},{6,4},{8,10},{10,8},{12,14},{14,12},{16,18},{18,... | collective-permute-start | bytes 589832 | tf_op jit(solution)/shard_map/ppermute | solution.py:213
  29.9 4.5 %collective-permute-start.11 = (bf16[96,1024]{1,0:T(8,128)(2,1)S(1)}, bf16[96,1024]{1,0:T(8,128)(2,1)S(1)}, u32[]{:S(2)}, u32[]{:S(2)}) collective-permute-start(bf16[96,1024]{1,0:T(8,128)(2,1)S(1)} %collective-permute-done.3.refs_12_), channel_id=1, source_target_pairs={{0,2},{2,0},{4,6},{6,4},{8,10},{10,8},{12,14},{14,12},{16,18},{18,... | collective-permute-start | bytes 589832 | tf_op jit(solution)/shard_map/ppermute | solution.py:213
  30.4 4.4 %collective-permute-start.13 = (bf16[96,1024]{1,0:T(8,128)(2,1)S(1)}, bf16[96,1024]{1,0:T(8,128)(2,1)S(1)}, u32[]{:S(2)}, u32[]{:S(2)}) collective-permute-start(bf16[96,1024]{1,0:T(8,128)(2,1)S(1)} %collective-permute-done.8.refs_14_), channel_id=1, source_target_pairs={{0,2},{2,0},{4,6},{6,4},{8,10},{10,8},{12,14},{14,12},{16,18},{18,... | collective-permute-start | bytes 589832 | tf_op jit(solution)/shard_map/ppermute | solution.py:213
  33.8 3.3 %collective-permute-start.5 = (bf16[96,1024]{1,0:T(8,128)(2,1)S(1)}, bf16[96,1024]{1,0:T(8,128)(2,1)S(1)}, u32[]{:S(2)}, u32[]{:S(2)}) collective-permute-start(bf16[96,1024]{1,0:T(8,128)(2,1)S(1)} %copy-done.2), channel_id=1, source_target_pairs={{0,2},{2,0},{4,6},{6,4},{8,10},{10,8},{12,14},{14,12},{16,18},{18,... | collective-permute-start | bytes 589832 | tf_op jit(solution)/shard_map/ppermute | solution.py:213
  33.8 3.3 %collective-permute-start.6 = (bf16[96,1024]{1,0:T(8,128)(2,1)S(1)}, bf16[96,1024]{1,0:T(8,128)(2,1)S(1)}, u32[]{:S(2)}, u32[]{:S(2)}) collective-permute-start(bf16[96,1024]{1,0:T(8,128)(2,1)S(1)} %collective-permute-done.refs_6_), channel_id=1, source_target_pairs={{0,2},{2,0},{4,6},{6,4},{8,10},{10,8},{12,14},{14,12},{16,18},{18,... | collective-permute-start | bytes 589832 | tf_op jit(solution)/shard_map/ppermute | solution.py:213
  34.3 2.8 %collective-permute-start.7 = (bf16[96,1024]{1,0:T(8,128)(2,1)S(1)}, bf16[96,1024]{1,0:T(8,128)(2,1)S(1)}, u32[]{:S(2)}, u32[]{:S(2)}) collective-permute-start(bf16[96,1024]{1,0:T(8,128)(2,1)S(1)} %collective-permute-done.1.refs_7_), channel_id=1, source_target_pairs={{0,2},{2,0},{4,6},{6,4},{8,10},{10,8},{12,14},{14,12},{16,18},{18,... | collective-permute-start | bytes 589832 | tf_op jit(solution)/shard_map/ppermute | solution.py:213
  34.4 2.7 %collective-permute-start.12 = (bf16[96,1024]{1,0:T(8,128)(2,1)S(1)}, bf16[96,1024]{1,0:T(8,128)(2,1)S(1)}, u32[]{:S(2)}, u32[]{:S(2)}) collective-permute-start(bf16[96,1024]{1,0:T(8,128)(2,1)S(1)} %collective-permute-done.4.refs_13_), channel_id=1, source_target_pairs={{0,2},{2,0},{4,6},{6,4},{8,10},{10,8},{12,14},{14,12},{16,18},{18,... | collective-permute-start | bytes 589832 | tf_op jit(solution)/shard_map/ppermute | solution.py:213
  34.8 6.2 %copy-start.4 = (bf16[1024,2048]{1,0:T(8,128)(2,1)S(1)}, bf16[1024,2048]{1,0:T(8,128)(2,1)}, u32[]{:S(2)}) copy-start(bf16[1024,2048]{1,0:T(8,128)(2,1)} %param.7) | copy-start | bytes 12582916
  34.8 22.4 %collective-permute-start.17 = (bf16[512,1024]{1,0:T(8,128)(2,1)}, bf16[512,1024]{1,0:T(8,128)(2,1)S(1)}, u32[]{:S(2)}, u32[]{:S(2)}) collective-permute-start(bf16[512,1024]{1,0:T(8,128)(2,1)} %copy-done.3), channel_id=1, source_target_pairs={{0,2},{2,4},{4,6},{6,8},{8,10},{10,12},{12,14},{14,16},{16,18},{18... | collective-permute-start | bytes 3145736 | tf_op jit(solution)/shard_map/ppermute | solution.py:234
  41.5 9.2 %collective-permute-start.15 = (bf16[128,1024]{1,0:T(8,128)(2,1)S(1)}, bf16[128,1024]{1,0:T(8,128)(2,1)S(1)}, u32[]{:S(2)}, u32[]{:S(2)}) collective-permute-start(bf16[128,1024]{1,0:T(8,128)(2,1)S(1)} %fusion.28), channel_id=1, source_target_pairs={{0,1},{1,0},{2,3},{3,2},{4,5},{5,4},{6,7},{7,6},{8,9},{9,8},{10,11... | collective-permute-start | bytes 786440 | tf_op jit(solution)/shard_map/ppermute | solution.py:259
  46.5 10.7 %collective-permute-start.16 = (bf16[128,1024]{1,0:T(8,128)(2,1)S(1)}, bf16[128,1024]{1,0:T(8,128)(2,1)S(1)}, u32[]{:S(2)}, u32[]{:S(2)}) collective-permute-start(bf16[128,1024]{1,0:T(8,128)(2,1)S(1)} %fusion.31), channel_id=1, source_target_pairs={{0,1},{1,0},{2,3},{3,2},{4,5},{5,4},{6,7},{7,6},{8,9},{9,8},{10,11... | collective-permute-start | bytes 786440 | tf_op jit(solution)/shard_map/ppermute | solution.py:259
  57.2 14.9 %collective-permute-start.19 = (bf16[256,1024]{1,0:T(8,128)(2,1)S(1)}, bf16[256,1024]{1,0:T(8,128)(2,1)S(1)}, u32[]{:S(2)}, u32[]{:S(2)}) collective-permute-start(bf16[256,1024]{1,0:T(8,128)(2,1)S(1)} %fusion.16), channel_id=1, source_target_pairs={{0,1},{1,0},{2,3},{3,2},{4,5},{5,4},{6,7},{7,6},{8,9},{9,8},{10,11... | collective-permute-start | bytes 1572872 | tf_op jit(solution)/shard_map/ppermute | solution.py:259
  57.3 1.0 %copy-start.5 = (bf16[512,1024]{1,0:T(8,128)(2,1)}, bf16[512,1024]{1,0:T(8,128)(2,1)S(1)}, u32[]{:S(2)}) copy-start(bf16[512,1024]{1,0:T(8,128)(2,1)S(1)} %collective-permute-done.17.refs_1_.refs_2_) | copy-start | bytes 3145732
  64.7 15.9 %collective-permute-start.18 = (bf16[256,1024]{1,0:T(8,128)(2,1)S(1)}, bf16[256,1024]{1,0:T(8,128)(2,1)S(1)}, u32[]{:S(2)}, u32[]{:S(2)}) collective-permute-start(bf16[256,1024]{1,0:T(8,128)(2,1)S(1)} %fusion.19), channel_id=1, source_target_pairs={{0,1},{1,0},{2,3},{3,2},{4,5},{5,4},{6,7},{7,6},{8,9},{9,8},{10,11... | collective-permute-start | bytes 1572872 | tf_op jit(solution)/shard_map/ppermute | solution.py:259
